TPU v7x, 512 devices: a whole 4x8x8 slice. The times are simulated.
512 devices in a mesh: slab: 64 (over x, z, core), dp: 8 (over y).
Axes of the slice: x: 4, y: 8, z: 8, core: 2. Of those that a mesh axis runs over, the one named last changes fastest.
Arguments:
- point_feats: float32 [8, 32768, 128], P('dp', 'slab'), may hold values from -6 to 6
- owner_slab: int32 [8, 32768, 1], P('dp', 'slab'), may hold values from 0 to 63; in each aligned block of 512 rows (0 to 511, 512 to 1023, ..., all dimensions but the last counted through in order) at most 16 rows name the same one
- block_slot: int32 [8, 32768], P('dp', 'slab'), may hold values from 0 to 1
- voxel_index: int32 [8, 32768], P('dp', 'slab'), may hold values from 0 to 511
- boundary: int32 [8, 64, 2, 1], P('dp', 'slab'), may hold values from 0 to 1, as said below
- neighbours: int32 [8, 128, 27], P('dp', 'slab'), may hold values from 0 to 4, as said below
- weight_taps: float32 [27, 128, 128], replicated, may hold values from -0.109375 to 0.109375
- cotangent: float32 [8, 65536, 128], P('dp', 'slab'), may hold values from -6 to 6
Outputs:
- activated: float32 [8, 65536, 128], P('dp', 'slab')
- point_grads: float32 [8, 32768, 128], P('dp', 'slab')
- weight_grads: float32 [3456, 128], P('slab')
Inputs may be any that keep to these rules, and one draw needn't show every extreme that they name: `owner_slab`: among the points of one device, no slab is named by more than 16 points, and exactly 16 in some device. `boundary`: each list of one slab holds 1 different block slots. `neighbours`: entry 13 of a block's row is the block's own slot. Entries 0 to 8 name a block of the slab (below 2), one of the 1 block from the slab before (2 to 2), or the zero block 4; entries 18 to 26 a block of the slab, one of the 1 block from the slab after, or the zero block; the others a block of the slab or the zero block.
All inputs are finite; a program needn't handle non-finite values.
Results may differ from a plain program's by a relative error of at most 0.0003.
Values sent between devices are 32-bit elements; how exact they have to be, the bound alone decides.
A program may use at most 64 MiB of HBM per device.

v0:
```python
import math

import jax
import jax.numpy as jnp
import numpy as np
from jax import lax
from jax.sharding import PartitionSpec as P

C = 128
E = 8
NB = 2
NH = 1
P_DEV = 512
VOX = 512


highest = lax.Precision.HIGHEST


def padded_2(value, sides, width):
    for axis, dim in sides:
        size, length = (lax.axis_size(axis), value.shape[dim])
        up = [(i, (i + 1) % size) for i in range(size)]
        down = [(j, i) for i, j in up]
        last = lax.slice_in_dim(value, length - width, length, axis=dim)
        leading = lax.slice_in_dim(value, 0, width, axis=dim)
        before = lax.ppermute(last, axis, up)
        after = lax.ppermute(leading, axis, down)
        value = jnp.concatenate([before, value, after], axis=dim)
    return value


def grid_tables():
    padded_edge = E + 2
    position = np.arange(padded_edge)
    section = np.where(position == 0, 0, np.where(position == padded_edge - 1, 2, 1))
    within = np.where(position == 0, E - 1, np.where(position == padded_edge - 1, 0, position - 1))
    grid_x, grid_y, grid_z = np.meshgrid(position, position, position, indexing="ij")
    tap_table = section[grid_x] * 9 + section[grid_y] * 3 + section[grid_z]
    voxel_table = within[grid_x] * E * E + within[grid_y] * E + within[grid_z]
    return (
        jnp.asarray(tap_table.reshape(-1), jnp.int32),
        jnp.asarray(voxel_table.reshape(-1), jnp.int32),
    )


def column_block(padded, tap_x):
    parts_list = [
        padded[:, tap_x : tap_x + E, tap_y : tap_y + E, tap_z : tap_z + E]
        for tap_y in range(3)
        for tap_z in range(3)
    ]
    return jnp.concatenate(parts_list, axis=-1).reshape(NB * VOX, 9 * C)


def per_device(
    point_feats, owner_slab, block_slot, voxel_index, boundary, neighbours, weight_taps, cotangent
):
    slabs = lax.axis_size("slab")
    windows = lax.axis_size("dp")
    capacity = 2 * P_DEV // slabs
    features = point_feats[0]
    target = owner_slab[0, :, 0]
    onehot = (target[:, None] == jnp.arange(slabs)[None, :]).astype(jnp.int32)
    ranks = jnp.sum((jnp.cumsum(onehot, axis=0) - onehot) * onehot, axis=1)
    placement = target * capacity + ranks
    send_rows = jnp.zeros((slabs * capacity, C), jnp.float32).at[placement].set(features)
    send_ids = (
        jnp.full((slabs * capacity,), -1, jnp.int32)
        .at[placement]
        .set(block_slot[0] * VOX + voxel_index[0])
    )
    recv_rows, recv_ids = (
        lax.all_to_all(
            send_rows.reshape(slabs, capacity, C), "slab", split_axis=0, concat_axis=0, tiled=True
        ),
        lax.all_to_all(
            send_ids.reshape(slabs, capacity), "slab", split_axis=0, concat_axis=0, tiled=True
        ),
    )
    flat_ids = recv_ids.reshape(-1)
    target_rows = jnp.where(flat_ids < 0, NB * VOX, flat_ids)
    voxel_feats = (
        jnp.zeros((NB * VOX + 1, C), jnp.float32)
        .at[target_rows]
        .add(recv_rows.reshape(-1, C))[: NB * VOX]
    )
    blocks = voxel_feats.reshape(NB, VOX, C)
    lend_left = boundary[0, 0, 0]
    lend_right = boundary[0, 0, 1]
    sent_left = blocks[lend_left]
    sent_right = blocks[lend_right]
    arrived = padded_2(jnp.stack((sent_left, sent_right)), (("slab", 0),), 1)
    from_left = arrived[0]
    from_right = arrived[3]
    slots_all = NB + 2 * NH + 1
    visible = jnp.concatenate(
        [blocks, from_left, from_right, jnp.zeros((1, VOX, C), jnp.float32)], axis=0
    )
    flat_visible = visible.reshape(slots_all * VOX, C)
    tap_table, voxel_table = grid_tables()
    gather_rows = neighbours[0][:, tap_table] * VOX + voxel_table[None, :]
    padded = flat_visible[gather_rows].reshape(NB, E + 2, E + 2, E + 2, C)
    pre_act = jnp.zeros((NB * VOX, C), jnp.float32)
    for tap_x in range(3):
        columns = column_block(padded, tap_x)
        group_weight = weight_taps[tap_x * 9 : tap_x * 9 + 9].reshape(9 * C, C)
        pre_act = pre_act + jnp.dot(
            columns, group_weight, precision=highest, preferred_element_type=jnp.float32
        )
    gate_value = jax.nn.sigmoid(pre_act)
    activated = pre_act * gate_value
    grad_pre = cotangent[0] * gate_value * (1.0 + pre_act * (1.0 - gate_value))
    pieces = []
    back_groups = []
    for tap_x in range(3):
        columns = column_block(padded, tap_x)
        pieces.append(
            lax.dot_general(
                columns,
                grad_pre,
                (((0,), (0,)), ((), ())),
                precision=highest,
                preferred_element_type=jnp.float32,
            )
        )
        group_back = weight_taps[tap_x * 9 : tap_x * 9 + 9].transpose(2, 0, 1).reshape(C, 9 * C)
        back_groups.append(
            jnp.dot(
                grad_pre, group_back, precision=highest, preferred_element_type=jnp.float32
            ).reshape(NB, E, E, E, 9, C)
        )
    weight_term = jnp.concatenate(pieces, axis=0)
    grad_padded = jnp.zeros((NB, E + 2, E + 2, E + 2, C), jnp.float32)
    for tap_x in range(3):
        for tap_y in range(3):
            for tap_z in range(3):
                shifted = back_groups[tap_x][:, :, :, :, tap_y * 3 + tap_z]
                grad_padded = grad_padded + jnp.pad(
                    shifted,
                    ((0, 0), (tap_x, 2 - tap_x), (tap_y, 2 - tap_y), (tap_z, 2 - tap_z), (0, 0)),
                )
    grad_visible = (
        jnp.zeros((slots_all * VOX, C), jnp.float32)
        .at[gather_rows.reshape(-1)]
        .add(grad_padded.reshape(-1, C))
    )
    grad_visible = grad_visible.reshape(slots_all, VOX, C)
    left_grads = grad_visible[NB : NB + NH]
    right_grads = grad_visible[NB + NH : NB + 2 * NH]
    returned = padded_2(jnp.stack((left_grads, right_grads)), (("slab", 0),), 1)
    for_lent_left = returned[0]
    for_lent_right = returned[3]
    grad_blocks = (
        grad_visible[:NB].at[lend_left].add(for_lent_left).at[lend_right].add(for_lent_right)
    )
    grad_flat = jnp.concatenate(
        [grad_blocks.reshape(NB * VOX, C), jnp.zeros((1, C), jnp.float32)], axis=0
    )
    back_points = grad_flat[target_rows].reshape(slabs, capacity, C)
    came_back = lax.all_to_all(back_points, "slab", split_axis=0, concat_axis=0, tiled=True)
    point_grads = came_back.reshape(slabs * capacity, C)[placement]
    share = lax.psum_scatter(weight_term, "slab", scatter_dimension=0, tiled=True)
    total = lax.psum(share, "dp")
    scale = 1.0 / math.sqrt(windows * slabs * NB * VOX)
    return (activated[None], point_grads[None], total * scale)


def solution(mesh):
    return jax.shard_map(
        per_device,
        mesh=mesh,
        in_specs=(
            P("dp", "slab", None),
            P("dp", "slab", None),
            P("dp", "slab"),
            P("dp", "slab"),
            P("dp", "slab", None, None),
            P("dp", "slab", None),
            P(),
            P("dp", "slab", None),
        ),
        out_specs=(P("dp", "slab", None), P("dp", "slab", None), P("slab", None)),
        check_vma=False,
    )
```

profile of v0, /device:TPU:4, one launch (start us, length us, event | category | flops | bytes accessed | tf_op | source)
XLA Modules:
  0.0 403.9 jit_solution(14868015423676881469)
XLA Ops:
  0.7 0.7 fusion.20
  1.4 1.2 reduce-window.6
  2.9 0.8 fusion.19
  3.7 0.7 compare_select_fusion.4
  4.4 0.7 multiply_add_fusion
  5.1 2.4 scatter_custom_fusion
  7.5 0.7 all_to_all.12
  8.2 13.9 %all-to-all-start = ((s32[64,1,16]{2,1,0:T(1,128)}), s32[64,1,16]{2,1,0:T(1,128)S(1)}, u32[]{:S(2)}, u32[]{:S(2)}) async-start(s32[64,1,16]{2,1,0:T(1,128)} %bitcast.7), calls=%async_computation | async-start | bytes 65536 | tf_op jit(solution)/shard_map/all_to_all | solution.py:77
  22.2 1.3 fusion.27
  26.1 2.7 fusion.26
  30.0 1.5 and_reduce_fusion
  31.5 0.8 copy.103
  32.3 2.5 scatter_custom_fusion.1
  34.9 10.3 %all-to-all-start.1 = ((f32[64,16,128]{2,1,0:T(8,128)}), f32[64,16,128]{2,1,0:T(8,128)S(1)}, u32[]{:S(2)}, u32[]{:S(2)}) async-start(f32[64,16,128]{2,1,0:T(8,128)} %bitcast.10), calls=%async_computation.1 | async-start | bytes 1048576 | tf_op jit(solution)/shard_map/all_to_all | solution.py:74
  45.7 0.7 reduce.21
  46.6 2.9 gather_fusion
  49.8 12.1 %all-to-all-done.1 = f32[64,16,128]{2,1,0:T(8,128)S(1)} async-done(((f32[64,16,128]{2,1,0:T(8,128)}), f32[64,16,128]{2,1,0:T(8,128)S(1)}, u32[]{:S(2)}, u32[]{:S(2)}) %all-to-all-start.1) | async-done | bytes 524320 | tf_op jit(solution)/shard_map/all_to_all | solution.py:74
  61.9 6.1 %scatter_custom_fusion.2 = f32[1025,128]{1,0:T(8,128)S(1)} fusion(s32[1024]{0:T(1024)S(1)} %bitcast.239, f32[1024,128]{1,0:T(8,128)S(1)} %bitcast.232, f32[]{:T(128)} %constant.74.clone.1), kind=kCustom, calls=%fused_computation.81 | custom fusion | flops 131072 | bytes 524804 | tf_op jit(solution)/shard_map/scatter-add | solution.py:86
  68.1 2.6 collective-permute-start
  70.7 5.1 %collective-permute-start.1 = (f32[1,1,512,128]{3,2,1,0:T(8,128)S(1)}, f32[1,1,512,128]{3,2,1,0:T(8,128)S(1)}, u32[]{:S(2)}, u32[]{:S(2)}) collective-permute-start(f32[1,1,512,128]{3,2,1,0:T(8,128)S(1)} %get-tuple-element.113), channel_id=1, source_target_pairs={{8,0},{16,8},{24,16},{32,24},{40,32},{48,40},{56,48},{64,56},{72,6... | collective-permute-start | bytes 786440 | tf_op jit(solution)/shard_map/ppermute | solution.py:28
  75.9 2.0 collective-permute-done
  77.9 1.8 collective-permute-done.1
  79.8 5.8 %gather_fusion.1 = f32[2000,128]{1,0:T(8,128)S(1)} fusion(f32[2560,128]{1,0:T(8,128)S(1)} %bitcast.213, s32[2048]{0:T(1024)S(1)} %pad_clamp_fusion), kind=kCustom, calls=%fused_computation.1 | custom fusion | bytes 2056000 | tf_op jit(solution)/shard_map/gather | solution.py:103
  88.0 4.1 %fusion.28 = f32[1024,128]{1,0:T(8,128)S(1)} fusion(f32[1024,1152]{1,0:T(8,128)S(1)} %bitcast.221, f32[1152,128]{1,0:T(8,128)S(1)} %bitcast.230), kind=kOutput, calls=%fused_computation.130 | convolution fusion | flops 1811939328 | bytes 5832704 | tf_op jit(solution)/shard_map/dot_general | solution.py:108
  92.1 4.1 %convolution_add_fusion.1 = f32[1024,128]{1,0:T(8,128)S(1)} fusion(f32[1024,128]{1,0:T(8,128)S(1)} %fusion.28, f32[1024,1152]{1,0:T(8,128)S(1)} %bitcast.219, f32[1152,128]{1,0:T(8,128)S(1)} %bitcast.229), kind=kOutput, calls=%fused_computation.12 | convolution fusion | flops 1812070400 | bytes 6356992 | tf_op jit(solution)/shard_map/dot_general | solution.py:108
  96.2 5.4 %fusion.9 = (f32[1024,128]{1,0:T(8,128)S(1)}, f32[1,1024,128]{2,1,0:T(8,128)}) fusion(f32[1,1024,128]{2,1,0:T(8,128)S(1)} %copy-done.7, f32[1024,128]{1,0:T(8,128)S(1)} %convolution_add_fusion.1, f32[1024,1152]{1,0:T(8,128)S(1)} %bitcast.217, f32[1152,128]{1,0:T(8,128)S(1)} %bitcast.228), kind=kOutput, calls=%fused_computation.76 | convolution fusion | flops 1813250048 | bytes 7405568 | tf_op jit(solution)/shard_map/dot_general | solution.py:108
  101.7 7.7 %fusion.29 = f32[1152,128]{1,0:T(8,128)S(1)} fusion(f32[1024,1152]{1,0:T(8,128)S(1)} %bitcast.222, f32[1024,128]{1,0:T(8,128)S(1)} %get-tuple-element.110), kind=kOutput, calls=%fused_computation.131 | convolution fusion | flops 1811939328 | bytes 5832704 | tf_op jit(solution)/shard_map/dot_general | solution.py:119
  109.4 8.7 %fusion.30 = f32[1152,128]{1,0:T(8,128)} fusion(f32[1024,1152]{1,0:T(8,128)S(1)} %bitcast.220, f32[1024,128]{1,0:T(8,128)S(1)} %get-tuple-element.110), kind=kOutput, calls=%fused_computation.132 | convolution fusion | flops 1811939328 | bytes 5832704 | tf_op jit(solution)/shard_map/dot_general | solution.py:119
  118.1 8.6 %fusion.31 = f32[1152,128]{1,0:T(8,128)} fusion(f32[1024,1152]{1,0:T(8,128)S(1)} %bitcast.218, f32[1024,128]{1,0:T(8,128)S(1)} %get-tuple-element.110), kind=kOutput, calls=%fused_computation.133 | convolution fusion | flops 1811939328 | bytes 5832704 | tf_op jit(solution)/shard_map/dot_general | solution.py:119
  126.7 4.2 %fusion.5 = f32[2,8,8,8,9,128]{5,3,2,1,0,4:T(8,128)S(1)} fusion(f32[2,8,8,8,128,1]{4,3,2,1,0,5:T(8,128)S(1)} %bitcast.214, f32[27,128,128]{2,1,0:T(8,128)S(1)} %copy-done.2), kind=kOutput, calls=%fused_computation.17 | convolution fusion | flops 1811939328 | bytes 5832704 | tf_op jit(solution)/shard_map/dot_general | solution.py:129
  130.9 3.8 fusion.3
  134.8 4.0 fusion.7
  139.5 0.7 slice_bitcast_fusion.17
  140.2 1.0 slice_bitcast_fusion.8
  141.1 2.9 pad_add_fusion
  144.1 1.1 reshape.431
  145.1 12.2 %scatter_custom_fusion.3 = f32[2560,128]{1,0:T(8,128)S(1)} fusion(s32[2000]{0:T(1024)S(1)} %bitcast.244, f32[2000,128]{1,0:T(8,128)} %reshape.431, f32[]{:T(128)} %constant.74.clone.1), kind=kCustom, calls=%fused_computation.13 | custom fusion | flops 256000 | bytes 1311232 | tf_op jit(solution)/shard_map/scatter-add | solution.py:146
  157.4 1.9 collective-permute-start.2
  159.3 5.9 %collective-permute-start.3 = (f32[1,1,512,128]{3,2,1,0:T(8,128)S(1)}, f32[1,1,512,128]{3,2,1,0:T(8,128)S(1)}, u32[]{:S(2)}, u32[]{:S(2)}) collective-permute-start(f32[1,1,512,128]{3,2,1,0:T(8,128)S(1)} %get-tuple-element.108), channel_id=1, source_target_pairs={{8,0},{16,8},{24,16},{32,24},{40,32},{48,40},{56,48},{64,56},{72,6... | collective-permute-start | bytes 786440 | tf_op jit(solution)/shard_map/ppermute | solution.py:28
  165.3 1.4 pad_maximum_fusion
  166.7 0.7 collective-permute-done.2
  167.3 0.7 fusion.12
  168.1 1.0 collective-permute-done.3
  169.1 0.7 fusion.13
  169.9 4.0 gather_fusion.2
  173.9 10.4 %all-to-all-start.2 = ((f32[64,16,128]{2,1,0:T(8,128)}), f32[64,16,128]{2,1,0:T(8,128)S(1)}, u32[]{:S(2)}, u32[]{:S(2)}) async-start(f32[64,16,128]{2,1,0:T(8,128)} %bitcast.231), calls=%async_computation.2 | async-start | bytes 1048576 | tf_op jit(solution)/shard_map/all_to_all | solution.py:161
  184.3 123.3 %fusion = f32[64,128]{1,0:T(8,128)S(1)} fusion(f32[3456,128]{1,0:T(8,128)S(1)} %pad_maximum_fusion), kind=kCustom, calls=%all-reduce-scatter | all-reduce-scatter fusion | flops 524289 | bytes 1804288
  307.6 1.9 collective-permute-start.10
  309.5 4.5 %collective-permute-start.11 = (f32[64,128]{1,0:T(8,128)S(1)}, f32[64,128]{1,0:T(8,128)S(1)}, u32[]{:S(2)}, u32[]{:S(2)}) collective-permute-start(f32[64,128]{1,0:T(8,128)S(1)} %fusion), channel_id=1, source_target_pairs={{0,64},{8,72},{16,80},{24,88},{32,96},{40,104},{48,112},{56,120},{... | collective-permute-start | bytes 98312
  314.0 8.4 %collective-permute-start.12 = (f32[64,128]{1,0:T(8,128)S(1)}, f32[64,128]{1,0:T(8,128)S(1)}, u32[]{:S(2)}, u32[]{:S(2)}) collective-permute-start(f32[64,128]{1,0:T(8,128)S(1)} %fusion), channel_id=1, source_target_pairs={{0,72},{8,80},{16,88},{24,96},{32,104},{40,112},{48,120},{56,128},... | collective-permute-start | bytes 98312
  322.4 2.1 collective-permute-start.4
  324.5 10.3 %collective-permute-start.13 = (f32[54,128]{1,0:T(8,128)S(1)}, f32[54,128]{1,0:T(8,128)S(1)}, u32[]{:S(2)}, u32[]{:S(2)}) collective-permute-start(f32[54,128]{1,0:T(8,128)S(1)} %slice.419), channel_id=1, source_target_pairs={{0,80},{8,88},{16,96},{24,104},{32,112},{40,120},{48,128},{56,136}... | collective-permute-start | bytes 82952
  334.8 1.5 collective-permute-done.13
  336.3 7.7 %collective-permute-start.5 = (f32[64,128]{1,0:T(8,128)S(1)}, f32[64,128]{1,0:T(8,128)S(1)}, u32[]{:S(2)}, u32[]{:S(2)}) collective-permute-start(f32[64,128]{1,0:T(8,128)S(1)} %fusion), channel_id=1, source_target_pairs={{0,16},{8,24},{16,32},{24,40},{32,48},{40,56},{48,64},{56,72},{64,... | collective-permute-start | bytes 98312
  344.1 9.3 %collective-permute-start.6 = (f32[64,128]{1,0:T(8,128)S(1)}, f32[64,128]{1,0:T(8,128)S(1)}, u32[]{:S(2)}, u32[]{:S(2)}) collective-permute-start(f32[64,128]{1,0:T(8,128)S(1)} %fusion), channel_id=1, source_target_pairs={{0,24},{8,32},{16,40},{24,48},{32,56},{40,64},{48,72},{56,80},{64,... | collective-permute-start | bytes 98312
  353.4 3.1 collective-permute-start.7
  356.5 1.9 collective-permute-start.8
  358.4 3.1 collective-permute-start.9
  361.5 1.3 dynamic-slice.32
  363.5 2.8 collective-permute-done.8
  366.3 2.8 collective-permute-done.9
  369.2 1.6 concatenate.39
  370.8 30.4 %psum.7 = f32[54,128]{1,0:T(8,128)S(1)} all-reduce(f32[54,128]{1,0:T(8,128)S(1)} %constant_dynamic-slice_fusion), channel_id=1, replica_groups=mesh['slab'=64,'dp'=8] {'dp'}, use_global_device_ids=true, to_apply=%region_10.11 | all-reduce | flops 6912 | bytes 55296 | tf_op jit(solution)/shard_map/psum | solution.py:164
  401.8 1.6 gather_fusion.3
  (67 shorter events, 5.3 us)
Async XLA Ops:
  0.6 31.6 %copy-start = (f32[1,512,128]{2,1,0:T(8,128)S(1)}, f32[1,512,128]{2,1,0:T(8,128)}, u32[]{:S(2)}) copy-start(f32[1,512,128]{2,1,0:T(8,128)} %param.14) | copy-start | bytes 786436
  0.6 45.9 %copy-start.9 = (s32[1000]{0:T(1024)S(1)}, s32[1000]{0:T(1024)}, u32[]{:S(2)}) copy-start(s32[1000]{0:T(1024)} %constant.196) | copy-start | bytes 12004
  0.7 49.0 %copy-start.8 = (s32[1000]{0:T(1024)S(1)}, s32[1000]{0:T(1024)}, u32[]{:S(2)}) copy-start(s32[1000]{0:T(1024)} %constant.90.clone) | copy-start | bytes 12004
  8.2 26.6 %all-to-all-start = ((s32[64,1,16]{2,1,0:T(1,128)}), s32[64,1,16]{2,1,0:T(1,128)S(1)}, u32[]{:S(2)}, u32[]{:S(2)}) async-start(s32[64,1,16]{2,1,0:T(1,128)} %bitcast.7), calls=%async_computation | async-start | bytes 65536 | tf_op jit(solution)/shard_map/all_to_all | solution.py:77
  34.9 27.0 %all-to-all-start.1 = ((f32[64,16,128]{2,1,0:T(8,128)}), f32[64,16,128]{2,1,0:T(8,128)S(1)}, u32[]{:S(2)}, u32[]{:S(2)}) async-start(f32[64,16,128]{2,1,0:T(8,128)} %bitcast.10), calls=%async_computation.1 | async-start | bytes 1048576 | tf_op jit(solution)/shard_map/all_to_all | solution.py:74
  68.1 9.8 %collective-permute-start = (f32[1,1,512,128]{3,2,1,0:T(8,128)S(1)}, f32[1,1,512,128]{3,2,1,0:T(8,128)S(1)}, u32[]{:S(2)}, u32[]{:S(2)}) collective-permute-start(f32[1,1,512,128]{3,2,1,0:T(8,128)S(1)} %get-tuple-element.112), channel_id=1, source_target_pairs={{0,8},{8,16},{16,24},{24,32},{32,40},{40,48},{48,56},{56,64},{64,7... | collective-permute-start | bytes 786440 | tf_op jit(solution)/shard_map/ppermute | solution.py:27
  70.7 8.9 %collective-permute-start.1 = (f32[1,1,512,128]{3,2,1,0:T(8,128)S(1)}, f32[1,1,512,128]{3,2,1,0:T(8,128)S(1)}, u32[]{:S(2)}, u32[]{:S(2)}) collective-permute-start(f32[1,1,512,128]{3,2,1,0:T(8,128)S(1)} %get-tuple-element.113), channel_id=1, source_target_pairs={{8,0},{16,8},{24,16},{32,24},{40,32},{48,40},{56,48},{64,56},{72,6... | collective-permute-start | bytes 786440 | tf_op jit(solution)/shard_map/ppermute | solution.py:28
  86.9 1.1 copy-start.6
  87.3 4.8 %copy-start.5 = (f32[9,128,128]{2,1,0:T(8,128)S(1)}, f32[9,128,128]{2,1,0:T(8,128)}, u32[]{:S(2)}) copy-start(f32[9,128,128]{2,1,0:T(8,128)} %get-tuple-element.80) | copy-start | bytes 1769476
  88.0 8.2 %copy-start.4 = (f32[9,128,128]{2,1,0:T(8,128)S(1)}, f32[9,128,128]{2,1,0:T(8,128)}, u32[]{:S(2)}) copy-start(f32[9,128,128]{2,1,0:T(8,128)} %get-tuple-element.78) | copy-start | bytes 1769476
  88.0 8.2 %copy-start.7 = (f32[1,1024,128]{2,1,0:T(8,128)S(1)}, f32[1,1024,128]{2,1,0:T(8,128)}, u32[]{:S(2)}) copy-start(f32[1,1024,128]{2,1,0:T(8,128)} %param.21) | copy-start | bytes 1572868
  109.4 17.3 %copy-start.2 = (f32[27,128,128]{2,1,0:T(8,128)S(1)}, f32[27,128,128]{2,1,0:T(8,128)}, u32[]{:S(2)}) copy-start(f32[27,128,128]{2,1,0:T(8,128)} %param.20) | copy-start | bytes 5308420
  157.3 2.0 copy-start.3
  157.4 10.0 %collective-permute-start.2 = (f32[1,1,512,128]{3,2,1,0:T(8,128)S(1)}, f32[1,1,512,128]{3,2,1,0:T(8,128)S(1)}, u32[]{:S(2)}, u32[]{:S(2)}) collective-permute-start(f32[1,1,512,128]{3,2,1,0:T(8,128)S(1)} %get-tuple-element.109), channel_id=1, source_target_pairs={{0,8},{8,16},{16,24},{24,32},{32,40},{40,48},{48,56},{56,64},{64,7... | collective-permute-start | bytes 786440 | tf_op jit(solution)/shard_map/ppermute | solution.py:27
  159.3 9.8 %collective-permute-start.3 = (f32[1,1,512,128]{3,2,1,0:T(8,128)S(1)}, f32[1,1,512,128]{3,2,1,0:T(8,128)S(1)}, u32[]{:S(2)}, u32[]{:S(2)}) collective-permute-start(f32[1,1,512,128]{3,2,1,0:T(8,128)S(1)} %get-tuple-element.108), channel_id=1, source_target_pairs={{8,0},{16,8},{24,16},{32,24},{40,32},{48,40},{56,48},{64,56},{72,6... | collective-permute-start | bytes 786440 | tf_op jit(solution)/shard_map/ppermute | solution.py:28
  165.2 2.1 slice-start
  169.9 233.6 %copy-start.1 = (f32[1,512,128]{2,1,0:T(8,128)S(1)}, f32[1,512,128]{2,1,0:T(8,128)}, u32[]{:S(2)}) copy-start(f32[1,512,128]{2,1,0:T(8,128)} %param.14) | copy-start | bytes 786436
  173.9 227.9 %all-to-all-start.2 = ((f32[64,16,128]{2,1,0:T(8,128)}), f32[64,16,128]{2,1,0:T(8,128)S(1)}, u32[]{:S(2)}, u32[]{:S(2)}) async-start(f32[64,16,128]{2,1,0:T(8,128)} %bitcast.231), calls=%async_computation.2 | async-start | bytes 1048576 | tf_op jit(solution)/shard_map/all_to_all | solution.py:161
  307.6 36.5 %collective-permute-start.10 = (f32[64,128]{1,0:T(8,128)S(1)}, f32[64,128]{1,0:T(8,128)S(1)}, u32[]{:S(2)}, u32[]{:S(2)}) collective-permute-start(f32[64,128]{1,0:T(8,128)S(1)} %fusion), channel_id=1, source_target_pairs={{0,56},{8,64},{16,72},{24,80},{32,88},{40,96},{48,104},{56,112},{6... | collective-permute-start | bytes 98312
  309.5 43.8 %collective-permute-start.11 = (f32[64,128]{1,0:T(8,128)S(1)}, f32[64,128]{1,0:T(8,128)S(1)}, u32[]{:S(2)}, u32[]{:S(2)}) collective-permute-start(f32[64,128]{1,0:T(8,128)S(1)} %fusion), channel_id=1, source_target_pairs={{0,64},{8,72},{16,80},{24,88},{32,96},{40,104},{48,112},{56,120},{... | collective-permute-start | bytes 98312
  314.0 42.5 %collective-permute-start.12 = (f32[64,128]{1,0:T(8,128)S(1)}, f32[64,128]{1,0:T(8,128)S(1)}, u32[]{:S(2)}, u32[]{:S(2)}) collective-permute-start(f32[64,128]{1,0:T(8,128)S(1)} %fusion), channel_id=1, source_target_pairs={{0,72},{8,80},{16,88},{24,96},{32,104},{40,112},{48,120},{56,128},... | collective-permute-start | bytes 98312
  322.4 36.0 %collective-permute-start.4 = (f32[64,128]{1,0:T(8,128)S(1)}, f32[64,128]{1,0:T(8,128)S(1)}, u32[]{:S(2)}, u32[]{:S(2)}) collective-permute-start(f32[64,128]{1,0:T(8,128)S(1)} %fusion), channel_id=1, source_target_pairs={{0,8},{8,16},{16,24},{24,32},{32,40},{40,48},{48,56},{56,64},{64,7... | collective-permute-start | bytes 98312
  324.5 11.8 %collective-permute-start.13 = (f32[54,128]{1,0:T(8,128)S(1)}, f32[54,128]{1,0:T(8,128)S(1)}, u32[]{:S(2)}, u32[]{:S(2)}) collective-permute-start(f32[54,128]{1,0:T(8,128)S(1)} %slice.419), channel_id=1, source_target_pairs={{0,80},{8,88},{16,96},{24,104},{32,112},{40,120},{48,128},{56,136}... | collective-permute-start | bytes 82952
  336.3 27.2 %collective-permute-start.5 = (f32[64,128]{1,0:T(8,128)S(1)}, f32[64,128]{1,0:T(8,128)S(1)}, u32[]{:S(2)}, u32[]{:S(2)}) collective-permute-start(f32[64,128]{1,0:T(8,128)S(1)} %fusion), channel_id=1, source_target_pairs={{0,16},{8,24},{16,32},{24,40},{32,48},{40,56},{48,64},{56,72},{64,... | collective-permute-start | bytes 98312
  344.1 19.4 %collective-permute-start.6 = (f32[64,128]{1,0:T(8,128)S(1)}, f32[64,128]{1,0:T(8,128)S(1)}, u32[]{:S(2)}, u32[]{:S(2)}) collective-permute-start(f32[64,128]{1,0:T(8,128)S(1)} %fusion), channel_id=1, source_target_pairs={{0,24},{8,32},{16,40},{24,48},{32,56},{40,64},{48,72},{56,80},{64,... | collective-permute-start | bytes 98312
  353.4 10.1 %collective-permute-start.7 = (f32[64,128]{1,0:T(8,128)S(1)}, f32[64,128]{1,0:T(8,128)S(1)}, u32[]{:S(2)}, u32[]{:S(2)}) collective-permute-start(f32[64,128]{1,0:T(8,128)S(1)} %fusion), channel_id=1, source_target_pairs={{0,32},{8,40},{16,48},{24,56},{32,64},{40,72},{48,80},{56,88},{64,... | collective-permute-start | bytes 98312
  356.5 9.9 %collective-permute-start.8 = (f32[64,128]{1,0:T(8,128)S(1)}, f32[64,128]{1,0:T(8,128)S(1)}, u32[]{:S(2)}, u32[]{:S(2)}) collective-permute-start(f32[64,128]{1,0:T(8,128)S(1)} %fusion), channel_id=1, source_target_pairs={{0,40},{8,48},{16,56},{24,64},{32,72},{40,80},{48,88},{56,96},{64,... | collective-permute-start | bytes 98312
  358.4 10.8 %collective-permute-start.9 = (f32[64,128]{1,0:T(8,128)S(1)}, f32[64,128]{1,0:T(8,128)S(1)}, u32[]{:S(2)}, u32[]{:S(2)}) collective-permute-start(f32[64,128]{1,0:T(8,128)S(1)} %fusion), channel_id=1, source_target_pairs={{0,48},{8,56},{16,64},{24,72},{32,80},{40,88},{48,96},{56,104},{64... | collective-permute-start | bytes 98312
where the time goes:
time: 411 us; the launch traced here: 404 us
  blocking collectives  154 us (37%)
  starting transfers between devices  102 us (25%)
  matrix products  50.7 us (12%)
  local copies, waits for them, and re-layouts  34.7 us (8%)
  other arithmetic  31.3 us (8%)
  waiting for transfers between devices  24.8 us (6%)
  between operations  6.27 us (2%)
    unnamed x1, blocking collectives  123 us
    unnamed x10, starting transfers between devices  52.3 us
    psum x1, blocking collectives, per_device(): total = lax.psum(share, 'dp')  30.4 us
    dot_general x3, matrix products, per_device(): lax.dot_general(columns, grad_pre, (((0,), (0,)), ((), ())), precision=hi...  25 us
    all_to_all x1, starting transfers between devices, per_device(): lax.all_to_all(send_ids.reshape(slabs, capacity), 'slab', split_axis=0, c...  13.9 us
    dot_general x3, matrix products, per_device(): jnp.dot(columns, group_weight, precision=highest, preferred_element_type=...  13.6 us
    scatter-add x1, other arithmetic, per_device(): grad_visible = jnp.zeros((slots_all * VOX, C), jnp.float32).at[gather_row...  12.2 us
    dot_general x3, matrix products, per_device(): jnp.dot(grad_pre, group_back, precision=highest, preferred_element_type=j...  12.1 us
  transfers between devices with their start and end apart: 17, of which 8 were waited for; matrix products, arithmetic and copies ran while one was open for 35% of the time, Pallas kernels for 0%

commit v1 on v0

v1 whole, which is shorter than its diff:
```python
import functools
import math

import jax
import jax.numpy as jnp
from jax import lax
from jax.experimental import pallas as pl
from jax.experimental.pallas import tpu as pltpu
from jax.sharding import PartitionSpec as P

C = 128
E = 8
NB = 2
PTS = 512
VOX = 512
ROWS = NB * VOX
TAPS = 27
SLOTS = 2 * PTS
f32 = jnp.float32
bf16 = jnp.bfloat16
i32 = jnp.int32
MESH = pl.DeviceIdType.MESH
highest = lax.Precision.HIGHEST
LIMIT = 60 * 1024 * 1024
PLACES = {64: (4, 8, 2), 8: (2, 2, 2), 4: (2, 1, 2)}


def iota(shape, dim):
    return lax.broadcasted_iota(i32, shape, dim)


def split(v):
    hi = v.astype(bf16)
    return hi, (v - hi.astype(f32)).astype(bf16)


def hilo(v):
    return jnp.concatenate(split(v), axis=-1)


def onehot(where):
    return jnp.where(where, 1.0, 0.0).astype(bf16)


def fold(v):
    return v[:, :C] + v[:, C:]


def dot(a, b):
    return lax.dot_general(a, b, (((1,), (0,)), ((), ())), preferred_element_type=f32)


def column(row):
    return jnp.transpose(jnp.broadcast_to(row, (8, row.shape[1])))[:, 0:1]


def pack_points(n, me, feats, own, vid, sbuf, place, idrows):
    cap = SLOTS // n
    group = C // cap
    ownr = own[...].astype(f32)
    ownc = column(ownr)
    first = iota((PTS, PTS), 0) < iota((PTS, PTS), 1)
    same = (ownc == ownr) & first
    rank = jnp.sum(jnp.where(same, 1.0, 0.0), axis=0, keepdims=True)
    placed = ownr * cap + rank
    place[...] = placed
    x2 = hilo(feats[...])
    pick = onehot(iota((SLOTS, PTS), 0).astype(f32) == placed)
    rows = fold(dot(pick, x2))
    sbuf[:, 0:cap, :] = rows.reshape(n, cap, C)
    lane = iota((PTS, C), 1).astype(f32)
    shift = (lax.rem(me, group) * cap).astype(f32)
    to_lane = jnp.where(lane == column(rank) + shift, 1.0, 0.0)
    ids = vid[...].astype(f32) + 1.0
    to_dest = jnp.where(iota((n, PTS), 0).astype(f32) == ownr, ids, 0.0)
    idrows[...] = lax.dot_general(
        to_dest, to_lane, (((1,), (0,)), ((), ())), precision=highest, preferred_element_type=f32
    )

    def put(d, carry):
        sbuf[d, cap : cap + 1, :] = idrows[pl.ds(d, 1), :]
        return carry

    lax.fori_loop(0, n, put, 0)


def prepare_taps(w, wp):
    def step(t, carry):
        rows = pl.ds(pl.multiple_of(t * 384, 384), 384)
        wp[rows, :] = hilo(w[rows, :])
        return carry

    lax.fori_loop(0, 9, step, 0)


def voxelize(n, rbuf, ids8, x2s, vis):
    cap = SLOTS // n
    group = C // cap
    x2s[...] = hilo(rbuf[:, 0:cap, :].reshape(SLOTS, C))
    ids = rbuf[:, cap : cap + 1, :].reshape(8, group, 1, C).sum(axis=1)
    ids8[...] = ids - 1.0

    def step(t, carry):
        vox = (iota((256, C), 0) + t * 256).astype(f32)
        pick = jnp.concatenate([onehot(vox == ids8[r]) for r in range(8)], axis=1)
        rows = pl.ds(pl.multiple_of(t * 256, 256), 256)
        vis[rows, :] = fold(dot(pick, x2s[...]))
        return carry

    lax.fori_loop(0, 4, step, 0)


SEC_P = ((slice(0, 1), slice(7, 8)), (slice(1, 9), slice(0, 8)), (slice(9, 10), slice(0, 1)))


def sections():
    for i in range(3):
        for j in range(3):
            if i == 1 and j == 1:
                for p in range(8):
                    yield i, j, slice(p + 1, p + 2), slice(1, 9), slice(p, p + 1), slice(0, 8)
            else:
                (ps, xs), (qs, ys) = SEC_P[i], SEC_P[j]
                yield i, j, ps, qs, xs, ys


def build_windows(nb, vis, S):
    for i, j, ps, qs, xs, ys in sections():
        e = 9 * i + 3 * j
        parts = ([], [], [])
        for b in range(NB):
            mid = vis[nb[b, e + 1], xs, ys]
            low = vis[nb[b, e], xs, ys]
            high = vis[nb[b, e + 2], xs, ys]
            z = iota(mid.shape, 2)
            parts[0].append(jnp.roll(jnp.where(z == 7, low, mid), 1, axis=2))
            parts[1].append(mid)
            parts[2].append(jnp.roll(jnp.where(z == 0, high, mid), -1, axis=2))
        for k in range(3):
            hi, lo = split(jnp.concatenate(parts[k], axis=2))
            S[ps, qs, :, k * C : (k + 1) * C] = hi
            S[ps, qs, :, (3 + k) * C : (4 + k) * C] = lo


def forward(S, wp, cot, act, G4, GT):
    def step(m, carry):
        total = None
        for part in range(2):
            wins = []
            for i in range(3):
                for j in range(3):
                    win = S[pl.ds(2 * m + i, 2), j : j + 8, :, part * 384 : part * 384 + 384]
                    wins.append(win.reshape(256, 384))
            got = dot(jnp.concatenate(wins, axis=1), wp[...])
            total = got if total is None else total + got
        pre = fold(total).reshape(2, 8, 16, C)
        gate = 1.0 / (1.0 + jnp.exp(-pre))
        xs = pl.ds(2 * m, 2)
        out = pre * gate
        for b in range(NB):
            act[b, xs] = out[:, :, 8 * b : 8 * b + 8]
        up = jnp.concatenate([cot[b, xs] for b in range(NB)], axis=2)
        g = (up * gate * (1.0 + pre * (1.0 - gate))).reshape(256, C)
        hi, lo = split(g)
        rows = pl.ds(pl.multiple_of(256 * m, 256), 256)
        G4[rows, :] = jnp.concatenate([hi, hi, lo, lo], axis=1)
        gt = jnp.transpose(g)
        thi, tlo = split(gt)
        GT[m, 0:C, :] = thi
        GT[m, C : 2 * C, :] = tlo
        return carry

    lax.fori_loop(0, 4, step, 0)


def weight_grad(S, GT, dW, scale):
    def step(ij, carry):
        i, j = ij // 3, lax.rem(ij, 3)
        total = None
        for m in range(4):
            win = S[pl.ds(i + 2 * m, 2), pl.ds(j, 8)].reshape(256, 768)
            got = dot(GT[m], win)
            total = got if total is None else total + got
        both = total[:C] + total[C:]
        for k in range(3):
            one = both[:, k * C : (k + 1) * C] + both[:, (3 + k) * C : (4 + k) * C]
            rows = pl.ds(pl.multiple_of(ij * 384 + k * C, C), C)
            dW[rows, :] = jnp.transpose(one) * scale
        return carry

    lax.fori_loop(0, 9, step, 0)


def input_grad(G4, wp, A):
    A[...] = jnp.zeros_like(A)

    def step(ij, carry):
        i, j = ij // 3, lax.rem(ij, 3)
        w = wp[pl.ds(pl.multiple_of(ij * 384, 384), 384), :]
        w2 = jnp.concatenate([w, w], axis=1)
        for m in range(4):
            y = lax.dot_general(
                G4[m * 256 : (m + 1) * 256, :], w2, (((1,), (1,)), ((), ())), preferred_element_type=f32
            )
            for k in range(3):
                A[k, pl.ds(i + 2 * m, 2), pl.ds(j, 8)] += y[:, k * C : (k + 1) * C].reshape(2, 8, 16, C)
        return carry

    lax.fori_loop(0, 9, step, 0)


def carry_back(nb, A, grad, lent):
    grad[...] = jnp.zeros_like(grad)
    lent[...] = jnp.zeros_like(lent)
    for i, j, ps, qs, xs, ys in sections():
        e = 9 * i + 3 * j
        for b in range(NB):
            a0, a1, a2 = (A[k, ps, qs, 8 * b : 8 * b + 8, :] for k in range(3))
            z = iota(a0.shape, 2)
            a0 = jnp.roll(a0, -1, axis=2)
            a2 = jnp.roll(a2, 1, axis=2)
            mid = a1 + jnp.where(z == 7, 0.0, a0) + jnp.where(z == 0, 0.0, a2)
            low = jnp.where(z == 7, a0, 0.0)
            high = jnp.where(z == 0, a2, 0.0)

            def share(t):
                part = jnp.where(nb[b, e] == t, low, 0.0) + jnp.where(nb[b, e + 2] == t, high, 0.0)
                if i == 1 and j == 1:
                    return part + mid if t == b else part
                return part + jnp.where(nb[b, e + 1] == t, mid, 0.0)

            for t in range(NB):
                grad[t, xs, ys] += share(t)
            if i == 0:
                lent[0, ys] += share(2)[0]
            if i == 2:
                lent[1, ys] += share(3)[0]


def chunk_rows(n):
    return TAPS * C // n


def padded_rows(n):
    return -(-chunk_rows(n) // 8) * 8


def cut_chunks(n, dW, dwc):
    X, Z, K = PLACES[n]
    size, pad = chunk_rows(n), padded_rows(n)
    for d in range(n):
        dwc[d % K, d // K // Z, d // K % Z] = dW[size * d : size * d + pad, :]


def greet(n, wins, me, y, columns):
    barrier = pltpu.get_barrier_semaphore()

    def hello(o, carry):
        pl.semaphore_signal(barrier, inc=1, device_id=(lax.rem(me + o, n), y), device_id_type=MESH)
        return carry

    lax.fori_loop(1, n, hello, 0)
    if columns:

        def hello_y(o, carry):
            pl.semaphore_signal(barrier, inc=1, device_id=(me, lax.rem(y + o, wins)), device_id_type=MESH)
            return carry

        lax.fori_loop(1, wins, hello_y, 0)


def greeted(n, wins, columns):
    pl.semaphore_wait(pltpu.get_barrier_semaphore(), n - 1 + (wins - 1 if columns else 0))


def spread(n, me, y, src, dst, ssem, rsem):
    def send(o, carry):
        d = lax.rem(me + o, n)
        pltpu.make_async_remote_copy(
            src_ref=src.at[d], dst_ref=dst.at[me], send_sem=ssem, recv_sem=rsem, device_id=(d, y), device_id_type=MESH
        ).start()
        return carry

    lax.fori_loop(1, n, send, 0)


def all_of(count, ref, sem):
    pltpu.make_async_copy(ref.at[pl.ds(0, count)], ref.at[pl.ds(0, count)], sem).wait()


def arrive(n, wins, feats, own, vid, bnd, w, vis, halo, ids8, place, wp, sbuf, rbuf, idrows, x2s, hs, hr, sems):
    me, y = lax.axis_index("slab"), lax.axis_index("dp")
    greet(n, wins, me, y, False)
    pack_points(n, me, feats, own, vid, sbuf, place, idrows)
    greeted(n, wins, False)
    spread(n, me, y, sbuf, rbuf, sems.at[0], sems.at[1])
    rbuf[me] = sbuf[me]
    prepare_taps(w, wp)
    all_of(n - 1, rbuf, sems.at[1])
    voxelize(n, rbuf, ids8, x2s, vis)
    hs[0] = jnp.where(bnd[1] == 1, vis[VOX + 448 : VOX + 512, :], vis[448:512, :])
    hs[1] = jnp.where(bnd[0] == 1, vis[VOX : VOX + 64, :], vis[0:64, :])
    copies = exchange(n, me, y, hs, hr, sems)
    all_of(n - 1, sbuf, sems.at[0])
    for copy in copies:
        copy.wait()
    halo[...] = hr[...]


def exchange(n, me, y, hs, hr, sems):
    copies = []
    for side, to in ((0, lax.rem(me + 1, n)), (1, lax.rem(me + n - 1, n))):
        copy = pltpu.make_async_remote_copy(
            src_ref=hs.at[side],
            dst_ref=hr.at[side],
            send_sem=sems.at[2 + side],
            recv_sem=sems.at[4 + side],
            device_id=(to, y),
            device_id_type=MESH,
        )
        copy.start()
        copies.append(copy)
    return copies


def middle(n, scale, own, halo, cot, wp, nb, act, dwc, grad, lent, vis, S, G4, GT, dW, A):
    vis[0:2] = own[...]
    vis[2, 7:8] = halo[0:1]
    vis[3, 0:1] = halo[1:2]
    vis[4] = jnp.zeros((8, 8, 8, C), f32)
    build_windows(nb, vis, S)
    forward(S, wp, cot, act, G4, GT)
    weight_grad(S, GT, dW, scale)
    cut_chunks(n, dW, dwc)
    input_grad(G4, wp, A)
    carry_back(nb, A, grad, lent)


def leave(n, wins, dwc, grad, lent, bnd, ids8, place, pts, total, core_r, xs_, x_r, zs_, z_r, ys_, y_r, hr, gfull, x2s, sbuf, rbuf, sems, rsems):
    X, Z, K = PLACES[n]
    cap = SLOTS // n
    me, y = lax.axis_index("slab"), lax.axis_index("dp")
    core = lax.rem(me, K)
    z = lax.rem(me // K, Z)
    x = me // (K * Z)
    greet(n, wins, me, y, True)
    greeted(n, wins, True)
    copies = []
    for side, to in ((0, lax.rem(me + n - 1, n)), (1, lax.rem(me + 1, n))):
        copy = pltpu.make_async_remote_copy(
            src_ref=lent.at[side],
            dst_ref=hr.at[side],
            send_sem=sems.at[2 + side],
            recv_sem=sems.at[4 + side],
            device_id=(to, y),
            device_id_type=MESH,
        )
        copy.start()
        copies.append(copy)
    core_copy = pltpu.make_async_remote_copy(
        src_ref=dwc.at[1 - core], dst_ref=core_r, send_sem=rsems.at[0], recv_sem=rsems.at[1],
        device_id=(me + 1 - 2 * core, y), device_id_type=MESH,
    )
    core_copy.start()
    for copy in copies:
        copy.wait()
    gfull[...] = grad[...]
    for t in range(NB):
        gfull[t, 448:512, :] += jnp.where(bnd[1] == t, hr[0], 0.0)
        gfull[t, 0:64, :] += jnp.where(bnd[0] == t, hr[1], 0.0)
    x2s[...] = hilo(gfull[...].reshape(ROWS, C))

    def pick_rows(r, carry):
        idc = column(ids8[r])
        pick = onehot(iota((C, ROWS), 1).astype(f32) == idc)
        rows = fold(dot(pick, x2s[...]))
        per = C // cap
        sbuf[pl.ds(r * per, per)] = rows.reshape(per, cap, C)
        return carry

    lax.fori_loop(0, 8, pick_rows, 0)
    spread(n, me, y, sbuf, rbuf, sems.at[0], sems.at[1])
    rbuf[me] = sbuf[me]
    core_copy.wait()

    def add_core(i, carry):
        xs_[i] = dwc[core, i] + core_r[i]
        return carry

    lax.fori_loop(0, X, add_core, 0)

    def ring(size, at, place_of, src, dst, ssem, rsem):
        def send(o, carry):
            d = lax.rem(at + o, size)
            pltpu.make_async_remote_copy(
                src_ref=src.at[d], dst_ref=dst.at[o - 1], send_sem=ssem, recv_sem=rsem,
                device_id=place_of(d), device_id_type=MESH,
            ).start()
            return carry

        if size > 1:
            lax.fori_loop(1, size, send, 0)
            all_of(size - 1, dst, rsem)
            all_of(size - 1, dst, ssem)

    ring(X, x, lambda d: ((d * Z + z) * K + core, y), xs_, x_r, rsems.at[2], rsems.at[3])

    def add_x(i, carry):
        part = xs_[x, i]
        for o in range(X - 1):
            part = part + x_r[o, i]
        zs_[i] = part
        return carry

    lax.fori_loop(0, Z, add_x, 0)
    ring(Z, z, lambda d: ((x * Z + d) * K + core, y), zs_, z_r, rsems.at[4], rsems.at[5])
    part = zs_[z]
    for o in range(Z - 1):
        part = part + z_r[o]
    ys_[...] = part

    def send_y(o, carry):
        pltpu.make_async_remote_copy(
            src_ref=ys_, dst_ref=y_r.at[o - 1], send_sem=rsems.at[6], recv_sem=rsems.at[7],
            device_id=(me, lax.rem(y + o, wins)), device_id_type=MESH,
        ).start()
        return carry

    lax.fori_loop(1, wins, send_y, 0)
    all_of(wins - 1, y_r, rsems.at[7])
    all_of(wins - 1, y_r, rsems.at[6])
    part = ys_[...]
    for o in range(wins - 1):
        part = part + y_r[o]
    total[...] = part[: chunk_rows(n)]
    all_of(n - 1, rbuf, sems.at[1])
    all_of(n - 1, sbuf, sems.at[0])
    x2s[...] = hilo(rbuf[...].reshape(SLOTS, C))
    pick = onehot(iota((PTS, SLOTS), 1).astype(f32) == column(place[...]))
    pts[...] = fold(dot(pick, x2s[...]))


VM = pl.BlockSpec(memory_space=pltpu.VMEM)
SM = pl.BlockSpec(memory_space=pltpu.SMEM)


def shape(*dims, dtype=f32):
    return jax.ShapeDtypeStruct(dims, dtype)


def middle_call(n, scale, own, halo, cot, wp, nb):
    X, Z, K = PLACES[n]
    return pl.pallas_call(
        functools.partial(middle, n, scale),
        out_shape=(
            shape(NB, 8, 8, 8, C),
            shape(K, X, Z, padded_rows(n), C),
            shape(NB, 8, 8, 8, C),
            shape(2, 8, 8, C),
        ),
        in_specs=[VM] * 4 + [SM],
        out_specs=(VM,) * 4,
        scratch_shapes=[
            pltpu.VMEM((5, 8, 8, 8, C), f32),
            pltpu.VMEM((10, 10, 16, 6 * C), bf16),
            pltpu.VMEM((ROWS, 4 * C), bf16),
            pltpu.VMEM((4, 2 * C, 256), bf16),
            pltpu.VMEM((TAPS * C + 8, C), f32),
            pltpu.VMEM((3, 10, 10, 16, C), f32),
        ],
        compiler_params=pltpu.CompilerParams(vmem_limit_bytes=LIMIT),
        name="middle",
    )(own, halo, cot, wp, nb)


def per_device(n, wins, point_feats, owner_slab, block_slot, voxel_index, boundary, neighbours, weight_taps, cotangent):
    X, Z, K = PLACES[n]
    cap = SLOTS // n
    pad = padded_rows(n)
    bnd = boundary.reshape(2)
    vid = block_slot * VOX + voxel_index
    vis, halo, ids8, place, wp = pl.pallas_call(
        functools.partial(arrive, n, wins),
        out_shape=(shape(ROWS, C), shape(2, 64, C), shape(8, 1, C), shape(1, PTS), shape(TAPS * C, 2 * C, dtype=bf16)),
        in_specs=[VM, VM, VM, SM, VM],
        out_specs=(VM,) * 5,
        scratch_shapes=[
            pltpu.VMEM((n, cap + 1, C), f32),
            pltpu.VMEM((n, cap + 1, C), f32),
            pltpu.VMEM((n, C), f32),
            pltpu.VMEM((SLOTS, 2 * C), bf16),
            pltpu.VMEM((2, 64, C), f32),
            pltpu.VMEM((2, 64, C), f32),
            pltpu.SemaphoreType.DMA((6,)),
        ],
        compiler_params=pltpu.CompilerParams(vmem_limit_bytes=LIMIT, collective_id=0, has_side_effects=True),
        name="arrive",
    )(point_feats[0], owner_slab.reshape(1, PTS), vid, bnd, weight_taps.reshape(TAPS * C, C))
    scale = 1.0 / math.sqrt(wins * n * ROWS)
    act, dwc, grad, lent = middle_call(
        n, scale, vis.reshape(NB, 8, 8, 8, C), halo.reshape(2, 8, 8, C), cotangent.reshape(NB, 8, 8, 8, C), wp, neighbours[0]
    )
    pts, total = pl.pallas_call(
        functools.partial(leave, n, wins),
        out_shape=(shape(PTS, C), shape(chunk_rows(n), C)),
        in_specs=[VM, VM, VM, SM, VM, VM],
        out_specs=(VM,) * 2,
        scratch_shapes=[
            pltpu.VMEM((X, Z, pad, C), f32),
            pltpu.VMEM((X, Z, pad, C), f32),
            pltpu.VMEM((max(X - 1, 1), Z, pad, C), f32),
            pltpu.VMEM((Z, pad, C), f32),
            pltpu.VMEM((max(Z - 1, 1), pad, C), f32),
            pltpu.VMEM((pad, C), f32),
            pltpu.VMEM((max(wins - 1, 1), pad, C), f32),
            pltpu.VMEM((2, 64, C), f32),
            pltpu.VMEM((NB, VOX, C), f32),
            pltpu.VMEM((SLOTS, 2 * C), bf16),
            pltpu.VMEM((n, cap, C), f32),
            pltpu.VMEM((n, cap, C), f32),
            pltpu.SemaphoreType.DMA((6,)),
            pltpu.SemaphoreType.DMA((8,)),
        ],
        compiler_params=pltpu.CompilerParams(vmem_limit_bytes=LIMIT, collective_id=1, has_side_effects=True),
        name="leave",
    )(dwc, grad.reshape(NB, VOX, C), lent.reshape(2, 64, C), bnd, ids8, place)
    return act.reshape(1, ROWS, C), pts[None], total


def solution(mesh):
    n, wins = mesh.shape["slab"], mesh.shape["dp"]
    return jax.shard_map(
        functools.partial(per_device, n, wins),
        mesh=mesh,
        in_specs=(
            P("dp", "slab", None),
            P("dp", "slab", None),
            P("dp", "slab"),
            P("dp", "slab"),
            P("dp", "slab", None, None),
            P("dp", "slab", None),
            P(),
            P("dp", "slab", None),
        ),
        out_specs=(P("dp", "slab", None), P("dp", "slab", None), P("slab", None)),
        check_vma=False,
    )
```

time: 411 us -> 114 us (0.28)
  the two profiles are of different devices: /device:TPU:4 before, /device:TPU:1 now
where the time goes in v1:
time: 114 us
  Pallas kernels  109 us (96%)
  local copies, waits for them, and re-layouts  3.03 us (3%)
  other arithmetic  1.28 us (1%)
    pallas_call x1, Pallas kernels, per_device(): pl.pallas_call(functools.partial(leave, n, wins), out_shape=(shape(PTS, C...  50.7 us
    pallas_call x1, Pallas kernels, per_device(): pl.pallas_call(functools.partial(arrive, n, wins), out_shape=(shape(ROWS,...  36.1 us
    pallas_call x1, Pallas kernels, middle_call(): pl.pallas_call(functools.partial(middle, n, scale), out_shape=(shape(NB,...  21.9 us
    unnamed x2, local copies, waits for them, and re-layouts  3.03 us

profile of v1, /device:TPU:1, one launch (start us, length us, event | category | flops | bytes accessed | tf_op | source)
XLA Modules:
  0.0 113.7 jit_solution(16579625918247109618)
XLA Ops:
  0.6 1.3 %multiply_add_fusion.vid = s32[1,512]{1,0:T(1,128)} fusion(s32[1,512]{1,0:T(1,128)} %param.11, s32[1,512]{1,0:T(1,128)} %param.10), kind=kLoop, calls=%fused_computation | loop fusion | flops 1024 | bytes 6144 | tf_op jit(solution)/shard_map/add | solution.py:481
  1.9 36.1 %arrive.1 = (f32[1024,128]{1,0:T(8,128)}, f32[2,64,128]{2,1,0:T(8,128)}, f32[8,1,128]{2,1,0:T(1,128)}, f32[1,512]{1,0:T(1,128)}, bf16[3456,256]{1,0:T(8,128)(2,1)}) custom-call(f32[512,128]{1,0:T(8,128)} %bitcast.16, s32[1,512]{1,0:T(1,128)} %bitcast.20, s32[1,512]{1,0:T(1,128)} %multiply_add_fusion.vid, s32[2]{0:T(128)} %bitcast.21, f32[3456,128]{1,0:T(8,128)} %bitcast.12), custom_call_target="tpu_custom_call" | custom-call | tf_op jit(solution)/shard_map/arrive/pallas_call | solution.py:482
  38.0 21.9 %middle.1 = (f32[2,8,8,8,128]{4,3,2,1,0:T(8,128)}, f32[2,4,8,56,128]{4,3,2,1,0:T(8,128)}, f32[2,8,8,8,128]{4,3,2,1,0:T(8,128)}, f32[2,8,8,128]{3,2,1,0:T(8,128)}) custom-call(f32[2,8,8,8,128]{4,3,2,1,0:T(8,128)} %bitcast.15, f32[2,8,8,128]{3,2,1,0:T(8,128)} %bitcast.19, f32[2,8,8,8,128]{4,3,2,1,0:T(8,128)} %bitcast.13, ...), custom_call_target="tpu_custom_call" | custom-call | tf_op jit(solution)/shard_map/middle/pallas_call | solution.py:453
  60.0 50.7 %leave.1 = (f32[512,128]{1,0:T(8,128)}, f32[54,128]{1,0:T(8,128)}) custom-call(f32[2,4,8,56,128]{4,3,2,1,0:T(8,128)} %get-tuple-element.18.dwc, f32[2,512,128]{2,1,0:T(8,128)} %bitcast.14, f32[2,64,128]{2,1,0:T(8,128)} %bitcast.18, s32[2]{0:T(128)} %bitcast.22, f32[8,1,128]{2,1,0:T(1,128)} %get-tuple-element.21.ids8, f32[1,512]{1,0:T(1,128)} %get-tuple-element.22.place), custom_call_target="tpu_custom_call" | custom-call | tf_op jit(solution)/shard_map/leave/pallas_call | solution.py:503
  110.7 1.7 %copy.13 = f32[1,512,128]{2,1,0:T(8,128)} copy(f32[1,512,128]{2,1,0:T(8,128)} %bitcast.17) | data formatting | bytes 524288
  112.4 1.4 %copy.14 = f32[54,128]{1,0:T(8,128)} copy(f32[54,128]{1,0:T(8,128)} %get-tuple-element.30) | data formatting | bytes 55296

commit v2 on v1

--- a/solution.py
+++ b/solution.py
@@ -54,7 +54,7 @@
     return jnp.transpose(jnp.broadcast_to(row, (8, row.shape[1])))[:, 0:1]
 
 
-def pack_points(n, me, feats, own, vid, sbuf, place, idrows):
+def pack_points(n, me, feats, own, slot, vox, sbuf, place, idrows):
     cap = SLOTS // n
     group = C // cap
     ownr = own[...].astype(f32)
@@ -71,7 +71,7 @@
     lane = iota((PTS, C), 1).astype(f32)
     shift = (lax.rem(me, group) * cap).astype(f32)
     to_lane = jnp.where(lane == column(rank) + shift, 1.0, 0.0)
-    ids = vid[...].astype(f32) + 1.0
+    ids = (slot[...] * VOX + vox[...]).astype(f32) + 1.0
     to_dest = jnp.where(iota((n, PTS), 0).astype(f32) == ownr, ids, 0.0)
     idrows[...] = lax.dot_general(
         to_dest, to_lane, (((1,), (0,)), ((), ())), precision=highest, preferred_element_type=f32
@@ -103,8 +103,7 @@
     def step(t, carry):
         vox = (iota((256, C), 0) + t * 256).astype(f32)
         pick = jnp.concatenate([onehot(vox == ids8[r]) for r in range(8)], axis=1)
-        rows = pl.ds(pl.multiple_of(t * 256, 256), 256)
-        vis[rows, :] = fold(dot(pick, x2s[...]))
+        vis[t // 2, pl.ds(lax.rem(t, 2) * 4, 4)] = fold(dot(pick, x2s[...])).reshape(4, 8, 8, C)
         return carry
 
     lax.fori_loop(0, 4, step, 0)
@@ -113,8 +112,8 @@
 SEC_P = ((slice(0, 1), slice(7, 8)), (slice(1, 9), slice(0, 8)), (slice(9, 10), slice(0, 1)))
 
 
-def sections():
-    for i in range(3):
+def sections(which=(0, 1, 2)):
+    for i in which:
         for j in range(3):
             if i == 1 and j == 1:
                 for p in range(8):
@@ -124,8 +123,8 @@
                 yield i, j, ps, qs, xs, ys
 
 
-def build_windows(nb, vis, S):
-    for i, j, ps, qs, xs, ys in sections():
+def build_windows(nb, vis, S, which):
+    for i, j, ps, qs, xs, ys in sections(which):
         e = 9 * i + 3 * j
         parts = ([], [], [])
         for b in range(NB):
@@ -191,8 +190,9 @@
     lax.fori_loop(0, 9, step, 0)
 
 
-def input_grad(G4, wp, A):
-    A[...] = jnp.zeros_like(A)
+def input_grad(G4, wp, A, first, last):
+    if first == 0:
+        A[...] = jnp.zeros_like(A)
 
     def step(ij, carry):
         i, j = ij // 3, lax.rem(ij, 3)
@@ -206,7 +206,7 @@
                 A[k, pl.ds(i + 2 * m, 2), pl.ds(j, 8)] += y[:, k * C : (k + 1) * C].reshape(2, 8, 16, C)
         return carry
 
-    lax.fori_loop(0, 9, step, 0)
+    lax.fori_loop(first, last, step, 0)
 
 
 def carry_back(nb, A, grad, lent):
@@ -287,35 +287,16 @@
 def all_of(count, ref, sem):
     pltpu.make_async_copy(ref.at[pl.ds(0, count)], ref.at[pl.ds(0, count)], sem).wait()
 
-
-def arrive(n, wins, feats, own, vid, bnd, w, vis, halo, ids8, place, wp, sbuf, rbuf, idrows, x2s, hs, hr, sems):
-    me, y = lax.axis_index("slab"), lax.axis_index("dp")
-    greet(n, wins, me, y, False)
-    pack_points(n, me, feats, own, vid, sbuf, place, idrows)
-    greeted(n, wins, False)
-    spread(n, me, y, sbuf, rbuf, sems.at[0], sems.at[1])
-    rbuf[me] = sbuf[me]
-    prepare_taps(w, wp)
-    all_of(n - 1, rbuf, sems.at[1])
-    voxelize(n, rbuf, ids8, x2s, vis)
-    hs[0] = jnp.where(bnd[1] == 1, vis[VOX + 448 : VOX + 512, :], vis[448:512, :])
-    hs[1] = jnp.where(bnd[0] == 1, vis[VOX : VOX + 64, :], vis[0:64, :])
-    copies = exchange(n, me, y, hs, hr, sems)
-    all_of(n - 1, sbuf, sems.at[0])
-    for copy in copies:
-        copy.wait()
-    halo[...] = hr[...]
-
-
-def exchange(n, me, y, hs, hr, sems):
+def both_ways(n, me, y, src, dst, sems, turn):
     copies = []
-    for side, to in ((0, lax.rem(me + 1, n)), (1, lax.rem(me + n - 1, n))):
+    for side in range(2):
+        step = 1 if (side == 0) != turn else n - 1
         copy = pltpu.make_async_remote_copy(
-            src_ref=hs.at[side],
-            dst_ref=hr.at[side],
-            send_sem=sems.at[2 + side],
-            recv_sem=sems.at[4 + side],
-            device_id=(to, y),
+            src_ref=src.at[side],
+            dst_ref=dst.at[side],
+            send_sem=sems.at[side],
+            recv_sem=sems.at[2 + side],
+            device_id=(lax.rem(me + step, n), y),
             device_id_type=MESH,
         )
         copy.start()
@@ -323,20 +304,13 @@
     return copies
 
 
-def middle(n, scale, own, halo, cot, wp, nb, act, dwc, grad, lent, vis, S, G4, GT, dW, A):
-    vis[0:2] = own[...]
-    vis[2, 7:8] = halo[0:1]
-    vis[3, 0:1] = halo[1:2]
-    vis[4] = jnp.zeros((8, 8, 8, C), f32)
-    build_windows(nb, vis, S)
-    forward(S, wp, cot, act, G4, GT)
-    weight_grad(S, GT, dW, scale)
-    cut_chunks(n, dW, dwc)
-    input_grad(G4, wp, A)
-    carry_back(nb, A, grad, lent)
-
-
-def leave(n, wins, dwc, grad, lent, bnd, ids8, place, pts, total, core_r, xs_, x_r, zs_, z_r, ys_, y_r, hr, gfull, x2s, sbuf, rbuf, sems, rsems):
+def whole(
+    n, wins, scale,
+    feats, own, slot, vox, bnd, nb, w, cot,
+    act, back, place, parts,
+    sbuf, rbuf, idrows, ids8, x2s, vis, hs, hr, wp, S, G4, GT, dW, A, grad, lent, lent_r, bbuf,
+    dwc, core_r, xs_, x_r, zs_, z_r, psems, hsems, bsems, qsems, rsems,
+):
     X, Z, K = PLACES[n]
     cap = SLOTS // n
     me, y = lax.axis_index("slab"), lax.axis_index("dp")
@@ -344,43 +318,33 @@
     z = lax.rem(me // K, Z)
     x = me // (K * Z)
     greet(n, wins, me, y, True)
+    pack_points(n, me, feats, own, slot, vox, sbuf, place, idrows)
     greeted(n, wins, True)
-    copies = []
-    for side, to in ((0, lax.rem(me + n - 1, n)), (1, lax.rem(me + 1, n))):
-        copy = pltpu.make_async_remote_copy(
-            src_ref=lent.at[side],
-            dst_ref=hr.at[side],
-            send_sem=sems.at[2 + side],
-            recv_sem=sems.at[4 + side],
-            device_id=(to, y),
-            device_id_type=MESH,
-        )
-        copy.start()
-        copies.append(copy)
+    spread(n, me, y, sbuf, rbuf, psems.at[0], psems.at[1])
+    rbuf[me] = sbuf[me]
+    prepare_taps(w, wp)
+    vis[4] = jnp.zeros((8, 8, 8, C), f32)
+    all_of(n - 1, rbuf, psems.at[1])
+    voxelize(n, rbuf, ids8, x2s, vis)
+    hs[0] = jnp.where(bnd[1] == 1, vis[1, 7], vis[0, 7])
+    hs[1] = jnp.where(bnd[0] == 1, vis[1, 0], vis[0, 0])
+    copies = both_ways(n, me, y, hs, hr, hsems, False)
+    build_windows(nb, vis, S, (1,))
+    all_of(n - 1, sbuf, psems.at[0])
+    for copy in copies:
+        copy.wait()
+    vis[2, 7] = hr[0]
+    vis[3, 0] = hr[1]
+    build_windows(nb, vis, S, (0, 2))
+    forward(S, wp, cot, act, G4, GT)
+    weight_grad(S, GT, dW, scale)
+    cut_chunks(n, dW, dwc)
     core_copy = pltpu.make_async_remote_copy(
         src_ref=dwc.at[1 - core], dst_ref=core_r, send_sem=rsems.at[0], recv_sem=rsems.at[1],
         device_id=(me + 1 - 2 * core, y), device_id_type=MESH,
     )
     core_copy.start()
-    for copy in copies:
-        copy.wait()
-    gfull[...] = grad[...]
-    for t in range(NB):
-        gfull[t, 448:512, :] += jnp.where(bnd[1] == t, hr[0], 0.0)
-        gfull[t, 0:64, :] += jnp.where(bnd[0] == t, hr[1], 0.0)
-    x2s[...] = hilo(gfull[...].reshape(ROWS, C))
-
-    def pick_rows(r, carry):
-        idc = column(ids8[r])
-        pick = onehot(iota((C, ROWS), 1).astype(f32) == idc)
-        rows = fold(dot(pick, x2s[...]))
-        per = C // cap
-        sbuf[pl.ds(r * per, per)] = rows.reshape(per, cap, C)
-        return carry
-
-    lax.fori_loop(0, 8, pick_rows, 0)
-    spread(n, me, y, sbuf, rbuf, sems.at[0], sems.at[1])
-    rbuf[me] = sbuf[me]
+    input_grad(G4, wp, A, 0, 4)
     core_copy.wait()
 
     def add_core(i, carry):
@@ -400,10 +364,33 @@
 
         if size > 1:
             lax.fori_loop(1, size, send, 0)
+
+    def ring_done(size, dst, ssem, rsem):
+        if size > 1:
             all_of(size - 1, dst, rsem)
             all_of(size - 1, dst, ssem)
 
     ring(X, x, lambda d: ((d * Z + z) * K + core, y), xs_, x_r, rsems.at[2], rsems.at[3])
+    input_grad(G4, wp, A, 4, 9)
+    carry_back(nb, A, grad, lent)
+    copies = both_ways(n, me, y, lent, lent_r, bsems, True)
+    for copy in copies:
+        copy.wait()
+    for t in range(NB):
+        grad[t, 7] += jnp.where(bnd[1] == t, lent_r[0], 0.0)
+        grad[t, 0] += jnp.where(bnd[0] == t, lent_r[1], 0.0)
+    x2s[...] = hilo(grad[...].reshape(ROWS, C))
+
+    def pick_rows(r, carry):
+        pick = onehot(iota((C, ROWS), 1).astype(f32) == column(ids8[r]))
+        per = C // cap
+        bbuf[pl.ds(r * per, per)] = fold(dot(pick, x2s[...])).reshape(per, cap, C)
+        return carry
+
+    lax.fori_loop(0, 8, pick_rows, 0)
+    spread(n, me, y, bbuf, back, qsems.at[0], qsems.at[1])
+    back[me] = bbuf[me]
+    ring_done(X, x_r, rsems.at[2], rsems.at[3])
 
     def add_x(i, carry):
         part = xs_[x, i]
@@ -414,30 +401,35 @@
 
     lax.fori_loop(0, Z, add_x, 0)
     ring(Z, z, lambda d: ((x * Z + d) * K + core, y), zs_, z_r, rsems.at[4], rsems.at[5])
+    ring_done(Z, z_r, rsems.at[4], rsems.at[5])
     part = zs_[z]
     for o in range(Z - 1):
         part = part + z_r[o]
-    ys_[...] = part
+    parts[wins - 1] = part
 
     def send_y(o, carry):
         pltpu.make_async_remote_copy(
-            src_ref=ys_, dst_ref=y_r.at[o - 1], send_sem=rsems.at[6], recv_sem=rsems.at[7],
+            src_ref=parts.at[wins - 1], dst_ref=parts.at[o - 1], send_sem=rsems.at[6], recv_sem=rsems.at[7],
             device_id=(me, lax.rem(y + o, wins)), device_id_type=MESH,
         ).start()
         return carry
 
     lax.fori_loop(1, wins, send_y, 0)
-    all_of(wins - 1, y_r, rsems.at[7])
-    all_of(wins - 1, y_r, rsems.at[6])
-    part = ys_[...]
-    for o in range(wins - 1):
-        part = part + y_r[o]
+    all_of(n - 1, back, qsems.at[1])
+    all_of(n - 1, bbuf, qsems.at[0])
+    all_of(wins - 1, parts, rsems.at[7])
+    all_of(wins - 1, parts, rsems.at[6])
+
+
+def finish(n, wins, act_in, back, place, parts, act, pts, total):
+    act[...] = act_in[...]
+    part = parts[0]
+    for o in range(1, wins):
+        part = part + parts[o]
     total[...] = part[: chunk_rows(n)]
-    all_of(n - 1, rbuf, sems.at[1])
-    all_of(n - 1, sbuf, sems.at[0])
-    x2s[...] = hilo(rbuf[...].reshape(SLOTS, C))
+    rows = hilo(back[...].reshape(SLOTS, C))
     pick = onehot(iota((PTS, SLOTS), 1).astype(f32) == column(place[...]))
-    pts[...] = fold(dot(pick, x2s[...]))
+    pts[...] = fold(dot(pick, rows))
 
 
 VM = pl.BlockSpec(memory_space=pltpu.VMEM)
@@ -446,85 +438,72 @@
 
 def shape(*dims, dtype=f32):
     return jax.ShapeDtypeStruct(dims, dtype)
-
-
-def middle_call(n, scale, own, halo, cot, wp, nb):
-    X, Z, K = PLACES[n]
-    return pl.pallas_call(
-        functools.partial(middle, n, scale),
-        out_shape=(
-            shape(NB, 8, 8, 8, C),
-            shape(K, X, Z, padded_rows(n), C),
-            shape(NB, 8, 8, 8, C),
-            shape(2, 8, 8, C),
-        ),
-        in_specs=[VM] * 4 + [SM],
-        out_specs=(VM,) * 4,
-        scratch_shapes=[
-            pltpu.VMEM((5, 8, 8, 8, C), f32),
-            pltpu.VMEM((10, 10, 16, 6 * C), bf16),
-            pltpu.VMEM((ROWS, 4 * C), bf16),
-            pltpu.VMEM((4, 2 * C, 256), bf16),
-            pltpu.VMEM((TAPS * C + 8, C), f32),
-            pltpu.VMEM((3, 10, 10, 16, C), f32),
-        ],
-        compiler_params=pltpu.CompilerParams(vmem_limit_bytes=LIMIT),
-        name="middle",
-    )(own, halo, cot, wp, nb)
 
 
 def per_device(n, wins, point_feats, owner_slab, block_slot, voxel_index, boundary, neighbours, weight_taps, cotangent):
     X, Z, K = PLACES[n]
     cap = SLOTS // n
     pad = padded_rows(n)
-    bnd = boundary.reshape(2)
-    vid = block_slot * VOX + voxel_index
-    vis, halo, ids8, place, wp = pl.pallas_call(
-        functools.partial(arrive, n, wins),
-        out_shape=(shape(ROWS, C), shape(2, 64, C), shape(8, 1, C), shape(1, PTS), shape(TAPS * C, 2 * C, dtype=bf16)),
-        in_specs=[VM, VM, VM, SM, VM],
-        out_specs=(VM,) * 5,
+    scale = 1.0 / math.sqrt(wins * n * ROWS)
+    vm = pltpu.VMEM
+    dma = pltpu.SemaphoreType.DMA
+    act, back, place, parts = pl.pallas_call(
+        functools.partial(whole, n, wins, scale),
+        out_shape=(shape(NB, 8, 8, 8, C), shape(n, cap, C), shape(1, PTS), shape(wins, pad, C)),
+        in_specs=[VM, VM, VM, VM, SM, SM, VM, VM],
+        out_specs=(VM,) * 4,
         scratch_shapes=[
-            pltpu.VMEM((n, cap + 1, C), f32),
-            pltpu.VMEM((n, cap + 1, C), f32),
-            pltpu.VMEM((n, C), f32),
-            pltpu.VMEM((SLOTS, 2 * C), bf16),
-            pltpu.VMEM((2, 64, C), f32),
-            pltpu.VMEM((2, 64, C), f32),
-            pltpu.SemaphoreType.DMA((6,)),
+            vm((n, cap + 1, C), f32),
+            vm((n, cap + 1, C), f32),
+            vm((n, C), f32),
+            vm((8, 1, C), f32),
+            vm((SLOTS, 2 * C), bf16),
+            vm((5, 8, 8, 8, C), f32),
+            vm((2, 8, 8, C), f32),
+            vm((2, 8, 8, C), f32),
+            vm((TAPS * C, 2 * C), bf16),
+            vm((10, 10, 16, 6 * C), bf16),
+            vm((ROWS, 4 * C), bf16),
+            vm((4, 2 * C, 256), bf16),
+            vm((TAPS * C + 8, C), f32),
+            vm((3, 10, 10, 16, C), f32),
+            vm((NB, 8, 8, 8, C), f32),
+            vm((2, 8, 8, C), f32),
+            vm((2, 8, 8, C), f32),
+            vm((n, cap, C), f32),
+            vm((K, X, Z, pad, C), f32),
+            vm((X, Z, pad, C), f32),
+            vm((X, Z, pad, C), f32),
+            vm((max(X - 1, 1), Z, pad, C), f32),
+            vm((Z, pad, C), f32),
+            vm((max(Z - 1, 1), pad, C), f32),
+            dma((2,)),
+            dma((4,)),
+            dma((4,)),
+            dma((2,)),
+            dma((8,)),
         ],
         compiler_params=pltpu.CompilerParams(vmem_limit_bytes=LIMIT, collective_id=0, has_side_effects=True),
-        name="arrive",
-    )(point_feats[0], owner_slab.reshape(1, PTS), vid, bnd, weight_taps.reshape(TAPS * C, C))
-    scale = 1.0 / math.sqrt(wins * n * ROWS)
-    act, dwc, grad, lent = middle_call(
-        n, scale, vis.reshape(NB, 8, 8, 8, C), halo.reshape(2, 8, 8, C), cotangent.reshape(NB, 8, 8, 8, C), wp, neighbours[0]
+        name="whole",
+    )(
+        point_feats[0],
+        owner_slab.reshape(1, PTS),
+        block_slot,
+        voxel_index,
+        boundary.reshape(2),
+        neighbours[0],
+        weight_taps.reshape(TAPS * C, C),
+        cotangent.reshape(NB, 8, 8, 8, C),
     )
-    pts, total = pl.pallas_call(
-        functools.partial(leave, n, wins),
-        out_shape=(shape(PTS, C), shape(chunk_rows(n), C)),
-        in_specs=[VM, VM, VM, SM, VM, VM],
-        out_specs=(VM,) * 2,
-        scratch_shapes=[
-            pltpu.VMEM((X, Z, pad, C), f32),
-            pltpu.VMEM((X, Z, pad, C), f32),
-            pltpu.VMEM((max(X - 1, 1), Z, pad, C), f32),
-            pltpu.VMEM((Z, pad, C), f32),
-            pltpu.VMEM((max(Z - 1, 1), pad, C), f32),
-            pltpu.VMEM((pad, C), f32),
-            pltpu.VMEM((max(wins - 1, 1), pad, C), f32),
-            pltpu.VMEM((2, 64, C), f32),
-            pltpu.VMEM((NB, VOX, C), f32),
-            pltpu.VMEM((SLOTS, 2 * C), bf16),
-            pltpu.VMEM((n, cap, C), f32),
-            pltpu.VMEM((n, cap, C), f32),
-            pltpu.SemaphoreType.DMA((6,)),
-            pltpu.SemaphoreType.DMA((8,)),
-        ],
-        compiler_params=pltpu.CompilerParams(vmem_limit_bytes=LIMIT, collective_id=1, has_side_effects=True),
-        name="leave",
-    )(dwc, grad.reshape(NB, VOX, C), lent.reshape(2, 64, C), bnd, ids8, place)
-    return act.reshape(1, ROWS, C), pts[None], total
+    act, pts, total = pl.pallas_call(
+        functools.partial(finish, n, wins),
+        out_shape=(shape(ROWS, C), shape(PTS, C), shape(chunk_rows(n), C)),
+        in_specs=[VM] * 4,
+        out_specs=(VM,) * 3,
+        compiler_params=pltpu.CompilerParams(vmem_limit_bytes=LIMIT),
+        name="finish",
+    )(act.reshape(ROWS, C), back, place, parts)
+    return act[None], pts[None], total
 
 
 def solution(mesh):

time: 114 us -> 93.1 us (0.82)
  the two profiles are of different devices: /device:TPU:1 before, /device:TPU:64 now
where the time goes in v2:
time: 93.1 us; the launch traced here: 93 us
  Pallas kernels  92.3 us (99%)
    pallas_call x1, Pallas kernels, per_device(): pl.pallas_call(functools.partial(whole, n, wins, scale), out_shape=(shape...  89.5 us
    pallas_call x1, Pallas kernels, per_device(): pl.pallas_call(functools.partial(finish, n, wins), out_shape=(shape(ROWS,...  2.8 us

profile of v2, /device:TPU:64, one launch (start us, length us, event | category | flops | bytes accessed | tf_op | source)
XLA Modules:
  0.0 93.0 jit_solution(1393296810343136318)
XLA Ops:
  0.6 89.5 %whole.1 = (f32[2,8,8,8,128]{4,3,2,1,0:T(8,128)}, f32[64,16,128]{2,1,0:T(8,128)}, f32[1,512]{1,0:T(1,128)}, f32[8,56,128]{2,1,0:T(8,128)}) custom-call(f32[512,128]{1,0:T(8,128)} %bitcast.12, s32[1,512]{1,0:T(1,128)} %bitcast.13, s32[1,512]{1,0:T(1,128)} %slot.1, s32[1,512]{1,0:T(1,128)} %vox.1, s32[2]{0:T(128)} %bitcast.15, s32[2,27]{1,0:T(2,128)} %bitcast.14, ...), custom_call_target="tpu_custom_call" | custom-call | tf_op jit(solution)/shard_map/whole/pallas_call | solution.py:450
  90.2 2.8 %finish.1 = (f32[1024,128]{1,0:T(8,128)}, f32[512,128]{1,0:T(8,128)}, f32[54,128]{1,0:T(8,128)}) custom-call(f32[1024,128]{1,0:T(8,128)} %bitcast.10, f32[64,16,128]{2,1,0:T(8,128)} %get-tuple-element.11.back, f32[1,512]{1,0:T(1,128)} %get-tuple-element.12.place, f32[8,56,128]{2,1,0:T(8,128)} %get-tuple-element.13.parts), custom_call_target="tpu_custom_call" | custom-call | tf_op jit(solution)/shard_map/finish/pallas_call | solution.py:498

commit v3 on v2

--- a/solution.py
+++ b/solution.py
@@ -172,7 +172,7 @@
     lax.fori_loop(0, 4, step, 0)
 
 
-def weight_grad(S, GT, dW, scale):
+def weight_grad(S, GT, dW, scale, first, last):
     def step(ij, carry):
         i, j = ij // 3, lax.rem(ij, 3)
         total = None
@@ -187,26 +187,34 @@
             dW[rows, :] = jnp.transpose(one) * scale
         return carry
 
-    lax.fori_loop(0, 9, step, 0)
+    lax.fori_loop(first, last, step, 0)
 
 
 def input_grad(G4, wp, A, first, last):
     if first == 0:
         A[...] = jnp.zeros_like(A)
 
-    def step(ij, carry):
-        i, j = ij // 3, lax.rem(ij, 3)
-        w = wp[pl.ds(pl.multiple_of(ij * 384, 384), 384), :]
+    def some(ij, count):
+        size = 384 * count
+        w = wp[pl.ds(pl.multiple_of(ij * 384, 384), size), :]
         w2 = jnp.concatenate([w, w], axis=1)
         for m in range(4):
             y = lax.dot_general(
                 G4[m * 256 : (m + 1) * 256, :], w2, (((1,), (1,)), ((), ())), preferred_element_type=f32
             )
-            for k in range(3):
-                A[k, pl.ds(i + 2 * m, 2), pl.ds(j, 8)] += y[:, k * C : (k + 1) * C].reshape(2, 8, 16, C)
-        return carry
-
-    lax.fori_loop(first, last, step, 0)
+            for c in range(count):
+                i, j = (ij + c) // 3, lax.rem(ij + c, 3)
+                for k in range(3):
+                    col = (3 * c + k) * C
+                    A[k, pl.ds(i + 2 * m, 2), pl.ds(j, 8)] += y[:, col : col + C].reshape(2, 8, 16, C)
+
+    def step(p, carry):
+        some(first + 2 * p, 2)
+        return carry
+
+    lax.fori_loop(0, (last - first) // 2, step, 0)
+    if (last - first) % 2:
+        some(last - 1, 1)
 
 
 def carry_back(nb, A, grad, lent):
@@ -245,14 +253,21 @@
     return -(-chunk_rows(n) // 8) * 8
 
 
-def cut_chunks(n, dW, dwc):
+def cut_chunks(n, dW, dwc, first, last):
     X, Z, K = PLACES[n]
     size, pad = chunk_rows(n), padded_rows(n)
-    for d in range(n):
+    for d in range(first, last):
         dwc[d % K, d // K // Z, d // K % Z] = dW[size * d : size * d + pad, :]
 
 
-def greet(n, wins, me, y, columns):
+def holders(n, wins):
+    tiles = padded_rows(n) // 8
+    return max(h for h in range(1, wins + 1) if tiles % h == 0)
+
+
+def greet(n, wins, me, y):
+    X, Z, K = PLACES[n]
+    core, z, x = lax.rem(me, K), lax.rem(me // K, Z), me // (K * Z)
     barrier = pltpu.get_barrier_semaphore()
 
     def hello(o, carry):
@@ -260,17 +275,17 @@
         return carry
 
     lax.fori_loop(1, n, hello, 0)
-    if columns:
-
-        def hello_y(o, carry):
-            pl.semaphore_signal(barrier, inc=1, device_id=(me, lax.rem(y + o, wins)), device_id_type=MESH)
-            return carry
-
-        lax.fori_loop(1, wins, hello_y, 0)
-
-
-def greeted(n, wins, columns):
-    pl.semaphore_wait(pltpu.get_barrier_semaphore(), n - 1 + (wins - 1 if columns else 0))
+
+    def hello_y(o, carry):
+        to = (x * Z + lax.rem(o, Z)) * K + core
+        pl.semaphore_signal(barrier, inc=1, device_id=(to, lax.rem(y + 1 + o // Z, wins)), device_id_type=MESH)
+        return carry
+
+    lax.fori_loop(0, Z * (wins - 1), hello_y, 0)
+
+
+def greeted(n, wins):
+    pl.semaphore_wait(pltpu.get_barrier_semaphore(), n - 1 + PLACES[n][1] * (wins - 1))
 
 
 def spread(n, me, y, src, dst, ssem, rsem):
@@ -306,24 +321,37 @@
 
 def whole(
     n, wins, scale,
-    feats, own, slot, vox, bnd, nb, w, cot,
-    act, back, place, parts,
-    sbuf, rbuf, idrows, ids8, x2s, vis, hs, hr, wp, S, G4, GT, dW, A, grad, lent, lent_r, bbuf,
-    dwc, core_r, xs_, x_r, zs_, z_r, psems, hsems, bsems, qsems, rsems,
+    feats, own, slot, vox, bnd, nb, w_in, cot_in,
+    act_out, back, place, tot,
+    w, cot, act, sbuf, rbuf, idrows, ids8, x2s, vis, hs, hr, wp, S, G4, GT, dW, A, grad, lent, lent_r, bbuf,
+    dwc, core_r, xs_, x_r, zs_, zy_r, lsems, psems, hsems, bsems, qsems, csems, rsems,
 ):
     X, Z, K = PLACES[n]
     cap = SLOTS // n
+    held = holders(n, wins)
     me, y = lax.axis_index("slab"), lax.axis_index("dp")
     core = lax.rem(me, K)
     z = lax.rem(me // K, Z)
     x = me // (K * Z)
-    greet(n, wins, me, y, True)
+
+    def remote(src, dst, ssem, rsem, slab, win):
+        return pltpu.make_async_remote_copy(
+            src_ref=src, dst_ref=dst, send_sem=ssem, recv_sem=rsem, device_id=(slab, win), device_id_type=MESH
+        )
+
+    w_copy = pltpu.make_async_copy(w_in, w, lsems.at[0])
+    cot_copy = pltpu.make_async_copy(cot_in, cot, lsems.at[1])
+    w_copy.start()
+    cot_copy.start()
+    greet(n, wins, me, y)
     pack_points(n, me, feats, own, slot, vox, sbuf, place, idrows)
-    greeted(n, wins, True)
+    greeted(n, wins)
     spread(n, me, y, sbuf, rbuf, psems.at[0], psems.at[1])
     rbuf[me] = sbuf[me]
+    vis[4] = jnp.zeros((8, 8, 8, C), f32)
+    w_copy.wait()
+    cot_copy.wait()
     prepare_taps(w, wp)
-    vis[4] = jnp.zeros((8, 8, 8, C), f32)
     all_of(n - 1, rbuf, psems.at[1])
     voxelize(n, rbuf, ids8, x2s, vis)
     hs[0] = jnp.where(bnd[1] == 1, vis[1, 7], vis[0, 7])
@@ -337,43 +365,79 @@
     vis[3, 0] = hr[1]
     build_windows(nb, vis, S, (0, 2))
     forward(S, wp, cot, act, G4, GT)
-    weight_grad(S, GT, dW, scale)
-    cut_chunks(n, dW, dwc)
-    core_copy = pltpu.make_async_remote_copy(
-        src_ref=dwc.at[1 - core], dst_ref=core_r, send_sem=rsems.at[0], recv_sem=rsems.at[1],
-        device_id=(me + 1 - 2 * core, y), device_id_type=MESH,
-    )
-    core_copy.start()
+    act_copy = pltpu.make_async_copy(act, act_out, lsems.at[2])
+    act_copy.start()
+
+    wide = X // 2
+
+    def half_of(h):
+        return pl.ds(h * wide, wide)
+
+    def core_start(h):
+        cut_chunks(n, dW, dwc, h * n // 2, (h + 1) * n // 2)
+        copy = remote(
+            dwc.at[1 - core, half_of(h)], core_r.at[half_of(h)], csems.at[h], csems.at[2 + h], me + 1 - 2 * core, y
+        )
+        copy.start()
+        return copy
+
+    def core_add(h):
+        def add_core(i, carry):
+            xs_[i] = dwc[core, i] + core_r[i]
+            return carry
+
+        lax.fori_loop(h * wide, (h + 1) * wide, add_core, 0)
+
+    def x_start(h):
+        def send(o, carry):
+            d = lax.rem(x + o, X)
+
+            @pl.when(d // wide == h)
+            def _():
+                remote(xs_.at[d], x_r.at[o - 1], rsems.at[0], rsems.at[1], (d * Z + z) * K + core, y).start()
+
+            return carry
+
+        lax.fori_loop(1, X, send, 0)
+
+    weight_grad(S, GT, dW, scale, 0, 5)
+    core_0 = core_start(0)
+    weight_grad(S, GT, dW, scale, 5, 9)
+    core_0.wait()
+    core_add(0)
+    x_start(0)
+    core_1 = core_start(1)
     input_grad(G4, wp, A, 0, 4)
-    core_copy.wait()
-
-    def add_core(i, carry):
-        xs_[i] = dwc[core, i] + core_r[i]
-        return carry
-
-    lax.fori_loop(0, X, add_core, 0)
-
-    def ring(size, at, place_of, src, dst, ssem, rsem):
-        def send(o, carry):
-            d = lax.rem(at + o, size)
-            pltpu.make_async_remote_copy(
-                src_ref=src.at[d], dst_ref=dst.at[o - 1], send_sem=ssem, recv_sem=rsem,
-                device_id=place_of(d), device_id_type=MESH,
-            ).start()
-            return carry
-
-        if size > 1:
-            lax.fori_loop(1, size, send, 0)
-
-    def ring_done(size, dst, ssem, rsem):
-        if size > 1:
-            all_of(size - 1, dst, rsem)
-            all_of(size - 1, dst, ssem)
-
-    ring(X, x, lambda d: ((d * Z + z) * K + core, y), xs_, x_r, rsems.at[2], rsems.at[3])
+    core_1.wait()
+    core_add(1)
+    x_start(1)
     input_grad(G4, wp, A, 4, 9)
     carry_back(nb, A, grad, lent)
     copies = both_ways(n, me, y, lent, lent_r, bsems, True)
+    all_of(X - 1, x_r, rsems.at[1])
+    all_of(X - 1, x_r, rsems.at[0])
+
+    def add_x(i, carry):
+        part = xs_[x, i]
+        for o in range(X - 1):
+            part = part + x_r[o, i]
+        zs_[i] = part.reshape(zs_.shape[1:])
+        return carry
+
+    lax.fori_loop(0, Z, add_x, 0)
+
+    def send_zy(o, carry):
+        zd, yd = lax.rem(z + o // held, Z), lax.rem(o, held)
+
+        @pl.when((o >= held) | (yd != y))
+        def _():
+            remote(
+                zs_.at[zd, yd], zy_r.at[z * wins + y], rsems.at[2], rsems.at[3], (x * Z + zd) * K + core, yd
+            ).start()
+
+        return carry
+
+    lax.fori_loop(0, Z * held, send_zy, 0)
     for copy in copies:
         copy.wait()
     for t in range(NB):
@@ -390,43 +454,42 @@
     lax.fori_loop(0, 8, pick_rows, 0)
     spread(n, me, y, bbuf, back, qsems.at[0], qsems.at[1])
     back[me] = bbuf[me]
-    ring_done(X, x_r, rsems.at[2], rsems.at[3])
-
-    def add_x(i, carry):
-        part = xs_[x, i]
-        for o in range(X - 1):
-            part = part + x_r[o, i]
-        zs_[i] = part
-        return carry
-
-    lax.fori_loop(0, Z, add_x, 0)
-    ring(Z, z, lambda d: ((x * Z + d) * K + core, y), zs_, z_r, rsems.at[4], rsems.at[5])
-    ring_done(Z, z_r, rsems.at[4], rsems.at[5])
-    part = zs_[z]
-    for o in range(Z - 1):
-        part = part + z_r[o]
-    parts[wins - 1] = part
-
-    def send_y(o, carry):
-        pltpu.make_async_remote_copy(
-            src_ref=parts.at[wins - 1], dst_ref=parts.at[o - 1], send_sem=rsems.at[6], recv_sem=rsems.at[7],
-            device_id=(me, lax.rem(y + o, wins)), device_id_type=MESH,
-        ).start()
-        return carry
-
-    lax.fori_loop(1, wins, send_y, 0)
+
+    @pl.when(y < held)
+    def _():
+        all_of(Z * wins - 1, zy_r, rsems.at[3])
+        zy_r[z * wins + y] = zs_[z, y]
+
+        def add_piece(o, part):
+            return part + zy_r[o]
+
+        tot[y] = lax.fori_loop(1, Z * wins, add_piece, zy_r[0])
+
+        def send_y(o, carry):
+            remote(tot.at[y], tot.at[y], rsems.at[4], rsems.at[5], me, lax.rem(y + o, wins)).start()
+            return carry
+
+        lax.fori_loop(1, wins, send_y, 0)
+
+    @pl.when(y < held)
+    def _():
+        all_of(Z * held - 1, zy_r, rsems.at[2])
+        all_of(held - 1, tot, rsems.at[5])
+        all_of(wins - 1, zy_r, rsems.at[4])
+
+    @pl.when(y >= held)
+    def _():
+        all_of(Z * held, zy_r, rsems.at[2])
+        all_of(held, tot, rsems.at[5])
+
     all_of(n - 1, back, qsems.at[1])
     all_of(n - 1, bbuf, qsems.at[0])
-    all_of(wins - 1, parts, rsems.at[7])
-    all_of(wins - 1, parts, rsems.at[6])
-
-
-def finish(n, wins, act_in, back, place, parts, act, pts, total):
+    act_copy.wait()
+
+
+def finish(n, act_in, back, place, tot, act, pts, total):
     act[...] = act_in[...]
-    part = parts[0]
-    for o in range(1, wins):
-        part = part + parts[o]
-    total[...] = part[: chunk_rows(n)]
+    total[...] = tot[...].reshape(padded_rows(n), C)[: chunk_rows(n)]
     rows = hilo(back[...].reshape(SLOTS, C))
     pick = onehot(iota((PTS, SLOTS), 1).astype(f32) == column(place[...]))
     pts[...] = fold(dot(pick, rows))
@@ -434,6 +497,7 @@
 
 VM = pl.BlockSpec(memory_space=pltpu.VMEM)
 SM = pl.BlockSpec(memory_space=pltpu.SMEM)
+ANY = pl.BlockSpec(memory_space=pl.ANY)
 
 
 def shape(*dims, dtype=f32):
@@ -444,15 +508,20 @@
     X, Z, K = PLACES[n]
     cap = SLOTS // n
     pad = padded_rows(n)
+    held = holders(n, wins)
+    per = pad // held
     scale = 1.0 / math.sqrt(wins * n * ROWS)
     vm = pltpu.VMEM
     dma = pltpu.SemaphoreType.DMA
-    act, back, place, parts = pl.pallas_call(
+    act, back, place, tot = pl.pallas_call(
         functools.partial(whole, n, wins, scale),
-        out_shape=(shape(NB, 8, 8, 8, C), shape(n, cap, C), shape(1, PTS), shape(wins, pad, C)),
-        in_specs=[VM, VM, VM, VM, SM, SM, VM, VM],
-        out_specs=(VM,) * 4,
+        out_shape=(shape(NB, 8, 8, 8, C), shape(n, cap, C), shape(1, PTS), shape(held, per, C)),
+        in_specs=[VM, VM, VM, VM, SM, SM, ANY, ANY],
+        out_specs=(ANY, VM, VM, VM),
         scratch_shapes=[
+            vm((TAPS * C, C), f32),
+            vm((NB, 8, 8, 8, C), f32),
+            vm((NB, 8, 8, 8, C), f32),
             vm((n, cap + 1, C), f32),
             vm((n, cap + 1, C), f32),
             vm((n, C), f32),
@@ -474,14 +543,16 @@
             vm((K, X, Z, pad, C), f32),
             vm((X, Z, pad, C), f32),
             vm((X, Z, pad, C), f32),
-            vm((max(X - 1, 1), Z, pad, C), f32),
-            vm((Z, pad, C), f32),
-            vm((max(Z - 1, 1), pad, C), f32),
+            vm((X - 1, Z, pad, C), f32),
+            vm((Z, held, per, C), f32),
+            vm((Z * wins, per, C), f32),
+            dma((3,)),
             dma((2,)),
             dma((4,)),
             dma((4,)),
             dma((2,)),
-            dma((8,)),
+            dma((4,)),
+            dma((6,)),
         ],
         compiler_params=pltpu.CompilerParams(vmem_limit_bytes=LIMIT, collective_id=0, has_side_effects=True),
         name="whole",
@@ -496,13 +567,13 @@
         cotangent.reshape(NB, 8, 8, 8, C),
     )
     act, pts, total = pl.pallas_call(
-        functools.partial(finish, n, wins),
+        functools.partial(finish, n),
         out_shape=(shape(ROWS, C), shape(PTS, C), shape(chunk_rows(n), C)),
         in_specs=[VM] * 4,
         out_specs=(VM,) * 3,
         compiler_params=pltpu.CompilerParams(vmem_limit_bytes=LIMIT),
         name="finish",
-    )(act.reshape(ROWS, C), back, place, parts)
+    )(act.reshape(ROWS, C), back, place, tot)
     return act[None], pts[None], total
 
 

time: 93.1 us -> 88.4 us (0.950)
  the two profiles are of different devices: /device:TPU:64 before, /device:TPU:1 now
where the time goes in v3:
time: 88.4 us; the launch traced here: 87.8 us
  Pallas kernels  87.2 us (99%)
    pallas_call x1, Pallas kernels, per_device(): pl.pallas_call(functools.partial(whole, n, wins, scale), out_shape=(shape...  84.4 us
    pallas_call x1, Pallas kernels, per_device(): pl.pallas_call(functools.partial(finish, n), out_shape=(shape(ROWS, C), s...  2.75 us

profile of v3, /device:TPU:1, one launch (start us, length us, event | category | flops | bytes accessed | tf_op | source)
XLA Modules:
  0.0 87.8 jit_solution(4537369182107594614)
XLA Ops:
  0.6 84.4 %whole.1 = (f32[2,8,8,8,128]{4,3,2,1,0:T(8,128)}, f32[64,16,128]{2,1,0:T(8,128)}, f32[1,512]{1,0:T(1,128)}, f32[7,8,128]{2,1,0:T(8,128)}) custom-call(f32[512,128]{1,0:T(8,128)} %bitcast.12, s32[1,512]{1,0:T(1,128)} %bitcast.13, s32[1,512]{1,0:T(1,128)} %slot.1, s32[1,512]{1,0:T(1,128)} %vox.1, s32[2]{0:T(128)} %bitcast.15, s32[2,27]{1,0:T(2,128)} %bitcast.14, ...), custom_call_target="tpu_custom_call" | custom-call | tf_op jit(solution)/shard_map/whole/pallas_call | solution.py:516
  85.1 2.8 %finish.1 = (f32[1024,128]{1,0:T(8,128)}, f32[512,128]{1,0:T(8,128)}, f32[54,128]{1,0:T(8,128)}) custom-call(f32[1024,128]{1,0:T(8,128)} %bitcast.10, f32[64,16,128]{2,1,0:T(8,128)} %get-tuple-element.11.back, f32[1,512]{1,0:T(1,128)} %get-tuple-element.12.place, f32[7,8,128]{2,1,0:T(8,128)} %get-tuple-element.13.tot), custom_call_target="tpu_custom_call" | custom-call | tf_op jit(solution)/shard_map/finish/pallas_call | solution.py:569

commit v4 on v3

--- a/solution.py
+++ b/solution.py
@@ -257,12 +257,17 @@
     X, Z, K = PLACES[n]
     size, pad = chunk_rows(n), padded_rows(n)
     for d in range(first, last):
-        dwc[d % K, d // K // Z, d // K % Z] = dW[size * d : size * d + pad, :]
+        rows = dW[size * d : size * d + pad, :]
+        dwc[d % K, d // K // Z, d // K % Z] = rows.reshape(dwc.shape[3:])
 
 
 def holders(n, wins):
     tiles = padded_rows(n) // 8
     return max(h for h in range(1, wins + 1) if tiles % h == 0)
+
+
+def x_first(n, wins):
+    return -(-holders(n, wins) * 4 // 7)
 
 
 def greet(n, wins, me, y):
@@ -283,9 +288,17 @@
 
     lax.fori_loop(0, Z * (wins - 1), hello_y, 0)
 
+    def hello_x(o, carry):
+        to = (lax.rem(x + 1 + lax.rem(o, X - 1), X) * Z + z) * K + core
+        pl.semaphore_signal(barrier, inc=1, device_id=(to, lax.rem(y + 1 + o // (X - 1), wins)), device_id_type=MESH)
+        return carry
+
+    lax.fori_loop(0, (X - 1) * (wins - 1), hello_x, 0)
+
 
 def greeted(n, wins):
-    pl.semaphore_wait(pltpu.get_barrier_semaphore(), n - 1 + PLACES[n][1] * (wins - 1))
+    X, Z, K = PLACES[n]
+    pl.semaphore_wait(pltpu.get_barrier_semaphore(), n - 1 + (X - 1 + Z) * (wins - 1))
 
 
 def spread(n, me, y, src, dst, ssem, rsem):
@@ -322,13 +335,15 @@
 def whole(
     n, wins, scale,
     feats, own, slot, vox, bnd, nb, w_in, cot_in,
-    act_out, back, place, tot,
-    w, cot, act, sbuf, rbuf, idrows, ids8, x2s, vis, hs, hr, wp, S, G4, GT, dW, A, grad, lent, lent_r, bbuf,
-    dwc, core_r, xs_, x_r, zs_, zy_r, lsems, psems, hsems, bsems, qsems, csems, rsems,
+    act, back, place, tot,
+    w, cot, sbuf, rbuf, idrows, ids8, x2s, vis, hs, hr, wp, S, G4, GT, dW, A, grad, lent, lent_r, bbuf,
+    dwc, core_r, xs_, x_r, zs_, zy_r, f_r, xs2, xy_r, lsems, psems, hsems, bsems, qsems, csems, rsems,
 ):
     X, Z, K = PLACES[n]
     cap = SLOTS // n
     held = holders(n, wins)
+    front = x_first(n, wins)
+    rear = held - front
     me, y = lax.axis_index("slab"), lax.axis_index("dp")
     core = lax.rem(me, K)
     z = lax.rem(me // K, Z)
@@ -365,8 +380,6 @@
     vis[3, 0] = hr[1]
     build_windows(nb, vis, S, (0, 2))
     forward(S, wp, cot, act, G4, GT)
-    act_copy = pltpu.make_async_copy(act, act_out, lsems.at[2])
-    act_copy.start()
 
     wide = X // 2
 
@@ -394,11 +407,23 @@
 
             @pl.when(d // wide == h)
             def _():
-                remote(xs_.at[d], x_r.at[o - 1], rsems.at[0], rsems.at[1], (d * Z + z) * K + core, y).start()
+                remote(
+                    xs_.at[d, :, pl.ds(0, front)], x_r.at[o - 1], rsems.at[0], rsems.at[1], (d * Z + z) * K + core, y
+                ).start()
 
             return carry
 
         lax.fori_loop(1, X, send, 0)
+
+        def send_z(o, carry):
+            d = lax.rem(z + o, Z)
+            remote(
+                xs_.at[half_of(h), d, pl.ds(front, rear)], f_r.at[o - 1, half_of(h)], rsems.at[6], rsems.at[7],
+                (x * Z + d) * K + core, y,
+            ).start()
+            return carry
+
+        lax.fori_loop(1, Z, send_z, 0)
 
     weight_grad(S, GT, dW, scale, 0, 5)
     core_0 = core_start(0)
@@ -414,22 +439,42 @@
     input_grad(G4, wp, A, 4, 9)
     carry_back(nb, A, grad, lent)
     copies = both_ways(n, me, y, lent, lent_r, bsems, True)
+    x2s[...] = hilo(grad[...].reshape(ROWS, C))
+    per = C // cap
+
+    def pick_rows(r, carry):
+        pick = onehot(iota((C, ROWS), 1).astype(f32) == column(ids8[r]))
+        bbuf[pl.ds(r * per, per)] = fold(dot(pick, x2s[...])).reshape(per, cap, C)
+        return carry
+
+    lax.fori_loop(0, 8, pick_rows, 0)
+    all_of(Z - 1, f_r, rsems.at[7])
+    all_of(Z - 1, f_r, rsems.at[6])
     all_of(X - 1, x_r, rsems.at[1])
     all_of(X - 1, x_r, rsems.at[0])
 
     def add_x(i, carry):
-        part = xs_[x, i]
+        part = xs_[x, i, 0:front]
         for o in range(X - 1):
             part = part + x_r[o, i]
-        zs_[i] = part.reshape(zs_.shape[1:])
+        zs_[i] = part
         return carry
 
     lax.fori_loop(0, Z, add_x, 0)
 
+    def add_z(i, carry):
+        part = xs_[i, z, front:held]
+        for o in range(Z - 1):
+            part = part + f_r[o, i]
+        xs2[i] = part
+        return carry
+
+    lax.fori_loop(0, X, add_z, 0)
+
     def send_zy(o, carry):
-        zd, yd = lax.rem(z + o // held, Z), lax.rem(o, held)
-
-        @pl.when((o >= held) | (yd != y))
+        zd, yd = lax.rem(z + o // front, Z), lax.rem(o, front)
+
+        @pl.when((o >= front) | (yd != y))
         def _():
             remote(
                 zs_.at[zd, yd], zy_r.at[z * wins + y], rsems.at[2], rsems.at[3], (x * Z + zd) * K + core, yd
@@ -437,25 +482,56 @@
 
         return carry
 
-    lax.fori_loop(0, Z * held, send_zy, 0)
+    lax.fori_loop(0, Z * front, send_zy, 0)
+
+    def send_xy(o, carry):
+        xd, j = lax.rem(x + o // rear, X), lax.rem(o, rear)
+
+        @pl.when((o >= rear) | (front + j != y))
+        def _():
+            remote(
+                xs2.at[xd, j], xy_r.at[x * wins + y], rsems.at[8], rsems.at[9], (xd * Z + z) * K + core, front + j
+            ).start()
+
+        return carry
+
+    lax.fori_loop(0, X * rear, send_xy, 0)
     for copy in copies:
         copy.wait()
+    planes = []
     for t in range(NB):
-        grad[t, 7] += jnp.where(bnd[1] == t, lent_r[0], 0.0)
-        grad[t, 0] += jnp.where(bnd[0] == t, lent_r[1], 0.0)
-    x2s[...] = hilo(grad[...].reshape(ROWS, C))
-
-    def pick_rows(r, carry):
-        pick = onehot(iota((C, ROWS), 1).astype(f32) == column(ids8[r]))
-        per = C // cap
-        bbuf[pl.ds(r * per, per)] = fold(dot(pick, x2s[...])).reshape(per, cap, C)
-        return carry
-
-    lax.fori_loop(0, 8, pick_rows, 0)
-    spread(n, me, y, bbuf, back, qsems.at[0], qsems.at[1])
+        planes.append(jnp.where(bnd[0] == t, lent_r[1], 0.0).reshape(64, C))
+        planes.append(jnp.where(bnd[1] == t, lent_r[0], 0.0).reshape(64, C))
+    x2s[0:256] = hilo(jnp.concatenate(planes, axis=0))
+
+    def add_planes(o, carry):
+        r = lax.rem(o + me // per, 8)
+        lane = iota((C, 256), 1)
+        at = lane % 64 + (lane // 64 % 2) * 448 + lane // 128 * VOX
+        pick = onehot(at.astype(f32) == column(ids8[r]))
+        bbuf[pl.ds(r * per, per)] += fold(dot(pick, x2s[0:256])).reshape(per, cap, C)
+
+        def send(k, carry):
+            d = r * per + k
+
+            @pl.when(d != me)
+            def _():
+                remote(bbuf.at[d], back.at[me], qsems.at[0], qsems.at[1], d, y).start()
+
+            return carry
+
+        return lax.fori_loop(0, per, send, carry)
+
+    lax.fori_loop(0, 8, add_planes, 0)
     back[me] = bbuf[me]
-
-    @pl.when(y < held)
+    def send_y(o, carry):
+        remote(tot.at[y], tot.at[y], rsems.at[4], rsems.at[5], me, lax.rem(y + o, wins)).start()
+        return carry
+
+    in_front = y < front
+    in_rear = (y >= front) & (y < held)
+
+    @pl.when(in_front)
     def _():
         all_of(Z * wins - 1, zy_r, rsems.at[3])
         zy_r[z * wins + y] = zs_[z, y]
@@ -464,27 +540,46 @@
             return part + zy_r[o]
 
         tot[y] = lax.fori_loop(1, Z * wins, add_piece, zy_r[0])
-
-        def send_y(o, carry):
-            remote(tot.at[y], tot.at[y], rsems.at[4], rsems.at[5], me, lax.rem(y + o, wins)).start()
-            return carry
-
         lax.fori_loop(1, wins, send_y, 0)
 
+    @pl.when(in_rear)
+    def _():
+        all_of(X * wins - 1, xy_r, rsems.at[9])
+        xy_r[x * wins + y] = xs2[x, y - front]
+
+        def add_piece(o, part):
+            return part + xy_r[o]
+
+        tot[y] = lax.fori_loop(1, X * wins, add_piece, xy_r[0])
+        lax.fori_loop(1, wins, send_y, 0)
+
+    @pl.when(in_front)
+    def _():
+        all_of(Z * front - 1, zy_r, rsems.at[2])
+
+    @pl.when(y >= front)
+    def _():
+        all_of(Z * front, zy_r, rsems.at[2])
+
+    @pl.when(in_rear)
+    def _():
+        all_of(X * rear - 1, xy_r, rsems.at[8])
+
+    @pl.when((y < front) | (y >= held))
+    def _():
+        all_of(X * rear, xy_r, rsems.at[8])
+
     @pl.when(y < held)
     def _():
-        all_of(Z * held - 1, zy_r, rsems.at[2])
         all_of(held - 1, tot, rsems.at[5])
         all_of(wins - 1, zy_r, rsems.at[4])
 
     @pl.when(y >= held)
     def _():
-        all_of(Z * held, zy_r, rsems.at[2])
         all_of(held, tot, rsems.at[5])
 
     all_of(n - 1, back, qsems.at[1])
     all_of(n - 1, bbuf, qsems.at[0])
-    act_copy.wait()
 
 
 def finish(n, act_in, back, place, tot, act, pts, total):
@@ -510,17 +605,18 @@
     pad = padded_rows(n)
     held = holders(n, wins)
     per = pad // held
+    front = x_first(n, wins)
+    rear = held - front
     scale = 1.0 / math.sqrt(wins * n * ROWS)
     vm = pltpu.VMEM
     dma = pltpu.SemaphoreType.DMA
     act, back, place, tot = pl.pallas_call(
         functools.partial(whole, n, wins, scale),
-        out_shape=(shape(NB, 8, 8, 8, C), shape(n, cap, C), shape(1, PTS), shape(held, per, C)),
+        out_shape=(vm((NB, 8, 8, 8, C), f32), vm((n, cap, C), f32), vm((1, PTS), f32), vm((held, per, C), f32)),
         in_specs=[VM, VM, VM, VM, SM, SM, ANY, ANY],
-        out_specs=(ANY, VM, VM, VM),
+        out_specs=(VM,) * 4,
         scratch_shapes=[
             vm((TAPS * C, C), f32),
-            vm((NB, 8, 8, 8, C), f32),
             vm((NB, 8, 8, 8, C), f32),
             vm((n, cap + 1, C), f32),
             vm((n, cap + 1, C), f32),
@@ -540,19 +636,22 @@
             vm((2, 8, 8, C), f32),
             vm((2, 8, 8, C), f32),
             vm((n, cap, C), f32),
-            vm((K, X, Z, pad, C), f32),
-            vm((X, Z, pad, C), f32),
-            vm((X, Z, pad, C), f32),
-            vm((X - 1, Z, pad, C), f32),
-            vm((Z, held, per, C), f32),
+            vm((K, X, Z, held, per, C), f32),
+            vm((X, Z, held, per, C), f32),
+            vm((X, Z, held, per, C), f32),
+            vm((X - 1, Z, front, per, C), f32),
+            vm((Z, front, per, C), f32),
             vm((Z * wins, per, C), f32),
-            dma((3,)),
+            vm((Z - 1, X, rear, per, C), f32),
+            vm((X, rear, per, C), f32),
+            vm((X * wins, per, C), f32),
+            dma((2,)),
             dma((2,)),
             dma((4,)),
             dma((4,)),
             dma((2,)),
             dma((4,)),
-            dma((6,)),
+            dma((10,)),
         ],
         compiler_params=pltpu.CompilerParams(vmem_limit_bytes=LIMIT, collective_id=0, has_side_effects=True),
         name="whole",
@@ -571,7 +670,7 @@
         out_shape=(shape(ROWS, C), shape(PTS, C), shape(chunk_rows(n), C)),
         in_specs=[VM] * 4,
         out_specs=(VM,) * 3,
-        compiler_params=pltpu.CompilerParams(vmem_limit_bytes=LIMIT),
+        compiler_params=pltpu.CompilerParams(vmem_limit_bytes=LIMIT // 3),
         name="finish",
     )(act.reshape(ROWS, C), back, place, tot)
     return act[None], pts[None], total

time: 88.4 us -> 85.1 us (0.963)
  Pallas kernels: 87.2 us -> 84.3 us
    pallas_call x1, Pallas kernels: 84.4 us -> 82.7 us  [per_device(): pl.pallas_call(functools.partial(whole, n, wins, scale), out_shape=(vm((N...]
    pallas_call x1, Pallas kernels: 2.75 us -> 1.55 us  [per_device(): pl.pallas_call(functools.partial(finish, n), out_shape=(shape(ROWS, C), s...]
where the time goes in v4:
time: 85.1 us; the launch traced here: 84.9 us
  Pallas kernels  84.3 us (99%)
    pallas_call x1, Pallas kernels, per_device(): pl.pallas_call(functools.partial(whole, n, wins, scale), out_shape=(vm((N...  82.7 us

profile of v4, /device:TPU:1, one launch (start us, length us, event | category | flops | bytes accessed | tf_op | source)
XLA Modules:
  0.0 84.9 jit_solution(16432096271739457317)
XLA Ops:
  0.6 82.7 %whole.1 = (f32[2,8,8,8,128]{4,3,2,1,0:T(8,128)S(1)}, f32[64,16,128]{2,1,0:T(8,128)S(1)}, f32[1,512]{1,0:T(1,128)S(1)}, f32[7,8,128]{2,1,0:T(8,128)S(1)}) custom-call(f32[512,128]{1,0:T(8,128)} %bitcast.12, s32[1,512]{1,0:T(1,128)} %bitcast.13, s32[1,512]{1,0:T(1,128)} %slot.1, s32[1,512]{1,0:T(1,128)} %vox.1, s32[2]{0:T(128)} %bitcast.15, ...), custom_call_target="tpu_custom_call" | custom-call | tf_op jit(solution)/shard_map/whole/pallas_call | solution.py:613
  83.4 1.6 %finish.1 = (f32[1024,128]{1,0:T(8,128)}, f32[512,128]{1,0:T(8,128)}, f32[54,128]{1,0:T(8,128)}) custom-call(f32[1024,128]{1,0:T(8,128)S(1)} %bitcast.9, f32[64,16,128]{2,1,0:T(8,128)S(1)} %get-tuple-element.11.back, f32[1,512]{1,0:T(1,128)S(1)} %get-tuple-element.12.place, f32[7,8,128]{2,1,0:T(8,128)S(1)} %get-tuple-element.13.tot), custom_call_target="tpu_custom_call" | custom-call | tf_op jit(solution)/shard_map/finish/pallas_call | solution.py:668

commit v5 on v4

--- a/solution.py
+++ b/solution.py
@@ -54,7 +54,7 @@
     return jnp.transpose(jnp.broadcast_to(row, (8, row.shape[1])))[:, 0:1]
 
 
-def pack_points(n, me, feats, own, slot, vox, sbuf, place, idrows):
+def pack_points(n, me, feats, arrived, own, slot, vox, sbuf, place, idrows):
     cap = SLOTS // n
     group = C // cap
     ownr = own[...].astype(f32)
@@ -64,8 +64,9 @@
     rank = jnp.sum(jnp.where(same, 1.0, 0.0), axis=0, keepdims=True)
     placed = ownr * cap + rank
     place[...] = placed
+    pick = onehot(iota((SLOTS, PTS), 0).astype(f32) == placed)
+    arrived()
     x2 = hilo(feats[...])
-    pick = onehot(iota((SLOTS, PTS), 0).astype(f32) == placed)
     rows = fold(dot(pick, x2))
     sbuf[:, 0:cap, :] = rows.reshape(n, cap, C)
     lane = iota((PTS, C), 1).astype(f32)
@@ -334,9 +335,9 @@
 
 def whole(
     n, wins, scale,
-    feats, own, slot, vox, bnd, nb, w_in, cot_in,
+    feats_in, own, slot, vox, bnd, nb, w_in, cot_in,
     act, back, place, tot,
-    w, cot, sbuf, rbuf, idrows, ids8, x2s, vis, hs, hr, wp, S, G4, GT, dW, A, grad, lent, lent_r, bbuf,
+    feats, w, cot, sbuf, rbuf, idrows, ids8, x2s, vis, hs, hr, wp, S, G4, GT, dW, A, grad, lent, lent_r, bbuf,
     dwc, core_r, xs_, x_r, zs_, zy_r, f_r, xs2, xy_r, lsems, psems, hsems, bsems, qsems, csems, rsems,
 ):
     X, Z, K = PLACES[n]
@@ -356,10 +357,12 @@
 
     w_copy = pltpu.make_async_copy(w_in, w, lsems.at[0])
     cot_copy = pltpu.make_async_copy(cot_in, cot, lsems.at[1])
+    feats_copy = pltpu.make_async_copy(feats_in, feats, lsems.at[2])
+    feats_copy.start()
+    greet(n, wins, me, y)
     w_copy.start()
     cot_copy.start()
-    greet(n, wins, me, y)
-    pack_points(n, me, feats, own, slot, vox, sbuf, place, idrows)
+    pack_points(n, me, feats, feats_copy.wait, own, slot, vox, sbuf, place, idrows)
     greeted(n, wins)
     spread(n, me, y, sbuf, rbuf, psems.at[0], psems.at[1])
     rbuf[me] = sbuf[me]
@@ -613,9 +616,10 @@
     act, back, place, tot = pl.pallas_call(
         functools.partial(whole, n, wins, scale),
         out_shape=(vm((NB, 8, 8, 8, C), f32), vm((n, cap, C), f32), vm((1, PTS), f32), vm((held, per, C), f32)),
-        in_specs=[VM, VM, VM, VM, SM, SM, ANY, ANY],
+        in_specs=[ANY, VM, VM, VM, SM, SM, ANY, ANY],
         out_specs=(VM,) * 4,
         scratch_shapes=[
+            vm((PTS, C), f32),
             vm((TAPS * C, C), f32),
             vm((NB, 8, 8, 8, C), f32),
             vm((n, cap + 1, C), f32),
@@ -645,7 +649,7 @@
             vm((Z - 1, X, rear, per, C), f32),
             vm((X, rear, per, C), f32),
             vm((X * wins, per, C), f32),
-            dma((2,)),
+            dma((3,)),
             dma((2,)),
             dma((4,)),
             dma((4,)),

time: 85.1 us -> 85 us (level)
  no operation moved by 1% of the time
where the time goes in v5:
time: 85 us; the launch traced here: 84.8 us
  Pallas kernels  84.2 us (99%)
    pallas_call x1, Pallas kernels, per_device(): pl.pallas_call(functools.partial(whole, n, wins, scale), out_shape=(vm((N...  82.6 us

profile of v5, /device:TPU:1, one launch (start us, length us, event | category | flops | bytes accessed | tf_op | source)
XLA Modules:
  0.0 84.8 jit_solution(864272069230872110)
XLA Ops:
  0.6 82.6 %whole.1 = (f32[2,8,8,8,128]{4,3,2,1,0:T(8,128)S(1)}, f32[64,16,128]{2,1,0:T(8,128)S(1)}, f32[1,512]{1,0:T(1,128)S(1)}, f32[7,8,128]{2,1,0:T(8,128)S(1)}) custom-call(f32[512,128]{1,0:T(8,128)} %bitcast.12, s32[1,512]{1,0:T(1,128)} %bitcast.13, s32[1,512]{1,0:T(1,128)} %slot.1, s32[1,512]{1,0:T(1,128)} %vox.1, s32[2]{0:T(128)} %bitcast.15, ...), custom_call_target="tpu_custom_call" | custom-call | tf_op jit(solution)/shard_map/whole/pallas_call | solution.py:616
  83.3 1.6 %finish.1 = (f32[1024,128]{1,0:T(8,128)}, f32[512,128]{1,0:T(8,128)}, f32[54,128]{1,0:T(8,128)}) custom-call(f32[1024,128]{1,0:T(8,128)S(1)} %bitcast.9, f32[64,16,128]{2,1,0:T(8,128)S(1)} %get-tuple-element.11.back, f32[1,512]{1,0:T(1,128)S(1)} %get-tuple-element.12.place, f32[7,8,128]{2,1,0:T(8,128)S(1)} %get-tuple-element.13.tot), custom_call_target="tpu_custom_call" | custom-call | tf_op jit(solution)/shard_map/finish/pallas_call | solution.py:672
